TPU v7x, 128 devices: a whole 4x4x4 slice. The times are simulated.
128 devices in a mesh: ctx: 16 (over y, z_lo, core), fsdp: 8 (over x, z_hi).
Axes of the slice: x: 4, y: 4, z: 4 (z_hi: 2, z_lo: 2; z = z_hi * 2 + z_lo), core: 2. Of those that a mesh axis runs over, the one named last changes fastest.
Arguments:
- layer_input: bfloat16 [8, 2048, 1024], P('fsdp', 'ctx'), may hold values from -6 to 6
- segment_ids: int32 [8, 2048], P('fsdp', 'ctx'), may hold values from 0 to 2, as said below
- norm_gain: bfloat16 [1024], P('fsdp'), may hold values from 0.5 to 1.5
- w_query: bfloat16 [1024, 512], P('fsdp'), may hold values from -0.1875 to 0.1875
- w_key: bfloat16 [1024, 128], P('fsdp'), may hold values from -0.1875 to 0.1875
- w_value: bfloat16 [1024, 128], P('fsdp'), may hold values from -0.1875 to 0.1875
- w_attn_out: bfloat16 [512, 1024], P('fsdp'), may hold values from -0.75 to 0.75
- w_gate_z: bfloat16 [1024, 1536], P('fsdp'), may hold values from -0.1875 to 0.1875
- w_inner: bfloat16 [1024, 1792], P('fsdp'), may hold values from -0.1875 to 0.1875
- w_step: bfloat16 [1024, 24], P('fsdp'), may hold values from -0.1875 to 0.1875
- conv_weight: bfloat16 [4, 1792], P(None, 'fsdp'), may hold values from -3 to 3
- conv_bias: bfloat16 [1792], P('fsdp'), may hold values from -3 to 3
- step_bias: bfloat16 [24], P('fsdp'), may hold values from -6 to -2
- decay_log: bfloat16 [24], P('fsdp'), may hold values from -4 to 1
- skip_gain: bfloat16 [24], P('fsdp'), may hold values from 0.5 to 1.5
- mixer_gain: bfloat16 [1536], P('fsdp'), may hold values from 0.5 to 1.5
- w_mixer_out: bfloat16 [1536, 1024], P('fsdp'), may hold values from -0.3125 to 0.3125
- ffn_gain: bfloat16 [1024], P('fsdp'), may hold values from 0.5 to 1.5
- w_gate: bfloat16 [1024, 2048], P('fsdp'), may hold values from -0.1875 to 0.1875
- w_up: bfloat16 [1024, 2048], P('fsdp'), may hold values from -0.1875 to 0.1875
- w_down: bfloat16 [2048, 1024], P('fsdp'), may hold values from -0.125 to 0.125
- out_grad: bfloat16 [8, 2048, 1024], P('fsdp', 'ctx'), may hold values from -6 to 6
Outputs:
- layer_output: bfloat16 [8, 2048, 1024], P('fsdp', 'ctx')
- input_grad: float32 [8, 2048, 1024], P('fsdp', 'ctx')
- grad_norm_gain: float32 [1024], P('fsdp')
- grad_w_query: float32 [1024, 512], P('fsdp')
- grad_w_key: float32 [1024, 128], P('fsdp')
- grad_w_value: float32 [1024, 128], P('fsdp')
- grad_w_attn_out: float32 [512, 1024], P('fsdp')
- grad_w_gate_z: float32 [1024, 1536], P('fsdp')
- grad_w_inner: float32 [1024, 1792], P('fsdp')
- grad_w_step: float32 [1024, 24], P('fsdp')
- grad_conv_weight: float32 [4, 1792], P(None, 'fsdp')
- grad_conv_bias: float32 [1792], P('fsdp')
- grad_step_bias: float32 [24], P('fsdp')
- grad_decay_log: float32 [24], P('fsdp')
- grad_skip_gain: float32 [24], P('fsdp')
- grad_mixer_gain: float32 [1536], P('fsdp')
- grad_w_mixer_out: float32 [1536, 1024], P('fsdp')
- grad_ffn_gain: float32 [1024], P('fsdp')
- grad_w_gate: float32 [1024, 2048], P('fsdp')
- grad_w_up: float32 [1024, 2048], P('fsdp')
- grad_w_down: float32 [2048, 1024], P('fsdp')
Inputs may be any that keep to these rules, and one draw needn't show every extreme that they name: `segment_ids`: each row holds three documents numbered 0, 1, 2 in order: document 0 ends within the first 128 positions and document 2 begins within the last 128.
All inputs are finite; a program needn't handle non-finite values.
Results may differ from a plain program's by a relative error of at most 0.025.
Values may be sent and summed in bfloat16 or wider, within the bound.
A program may use at most 192 MiB of HBM per device.

v0:
```python
import jax
import jax.numpy as jnp
from jax import lax
from jax.experimental import pallas as pl
from jax.experimental.pallas import tpu as pltpu
from jax.sharding import PartitionSpec as P

HEADS = 8
KV_HEADS = 2
HEAD_DIM = 64
SSM_HEADS = 24
SSM_DIM = 64
STATE = 128
CONV = 4


epsilon = 1e-05
rope_base = 10000.0
key_scale = 0.5
attn_out_scale = 0.8
mixer_out_scale = 0.5
gate_scale = 0.75
down_scale = 0.8
masked_score = -1e30
highest = lax.Precision.HIGHEST


def matmul_f32(left_side, right_side):
    return jnp.dot(left_side, right_side, preferred_element_type=jnp.float32)


def right_trans(left_side, right_side):
    return lax.dot_general(
        left_side, right_side, (((1,), (1,)), ((), ())), preferred_element_type=jnp.float32
    )


def rms_scale(values, gain_vec):
    return (
        values * lax.rsqrt(jnp.mean(values * values, axis=-1, keepdims=True) + epsilon) * gain_vec
    )


MESH = pl.DeviceIdType.MESH
CTX = 16
FSDP = 8
COLS = 4352
PAD_AT = 4224
HALVES = {"one": 2176, "two": 2048, "three": 512}
UNIT_ROWS = {"one": 16, "two": 16, "three": 64}
ORDERS = (("x", "y", "z"), ("y", "z", "x"), ("z", "x", "y"))
CUTS = {
    "one": (((0, 16), (0, 768)), ((0, 16), (768, 1536)), ((0, 16), (1536, 2176))),
    "two": (((0, 16), (0, 256)), ((0, 16), (256, 1152)), ((0, 16), (1152, 2048))),
    "three": (((0, 32), (0, 512)), ((32, 48), (0, 512)), ((48, 64), (0, 512))),
}
OUT_ROWS = 512
EVERYTHING = ("x", "y", "z")
SMALL = 1577
WIDTH = SSM_DIM * SSM_HEADS
HALF_WIDTH = WIDTH // 2
CONV_WIDTH = WIDTH + 2 * STATE
VMEM_LIMIT = 60 * 2**20


def place():
    f, c = lax.axis_index("fsdp"), lax.axis_index("ctx")
    return f, c, c // 4, (c // 2) % 2, c % 2


def at_ctx(y, low_z, core):
    return (y * 2 + low_z) * 2 + core


def meet(partners):
    barrier = pltpu.get_barrier_semaphore()
    for partner in partners:
        pl.semaphore_signal(barrier, inc=1, device_id=partner, device_id_type=MESH)
    pl.semaphore_wait(barrier, len(partners))


class Sender:
    def __init__(self, send_sem, recv_sem):
        self.send_sem, self.recv_sem, self.used, self.all = send_sem, recv_sem, 0, []

    def push(self, src, dst, partner):
        index = self.used
        self.used += 1
        copy = pltpu.make_async_remote_copy(
            src_ref=src,
            dst_ref=dst,
            send_sem=self.send_sem.at[index],
            recv_sem=self.recv_sem.at[index],
            device_id=partner,
            device_id_type=MESH,
        )
        copy.start()
        self.all.append(copy)
        return copy

    def drain(self):
        for copy in self.all:
            copy.wait_send()


def call_kernel(body, name, cid, outs, ins, sems, scratch=(), far_in=(), far_out=(), aliases=None):
    def spec(far):
        return pl.BlockSpec(memory_space=pl.ANY if far else pltpu.VMEM)

    return pl.pallas_call(
        body,
        name=name,
        out_shape=outs,
        in_specs=[spec(k in far_in) for k in range(len(ins))],
        out_specs=tuple(spec(k in far_out) for k in range(len(outs))),
        scratch_shapes=[
            *scratch,
            pltpu.SemaphoreType.DMA((sems,)),
            pltpu.SemaphoreType.DMA((sems,)),
        ],
        input_output_aliases=aliases or {},
        compiler_params=pltpu.CompilerParams(
            collective_id=cid, has_side_effects=True, vmem_limit_bytes=VMEM_LIMIT
        ),
    )(*ins)


def shape_of(dims, kind):
    return jax.ShapeDtypeStruct(dims, kind)


AXES = (("x", "x"), ("zh", "z"), ("y", "y"), ("zl", "z"))
EXTENT = {"x": 4, "zh": 2, "y": 4, "zl": 2}


def coordinates():
    f, c, y, low_z, core = place()
    return {"x": f // 2, "zh": f % 2, "y": y, "zl": low_z}, core


def neighbours(here, core):
    z = here["zh"] * 2 + here["zl"]
    found = {"x": [], "y": [], "z": []}
    for e in range(1, 4):
        found["x"].append({**here, "x": (here["x"] + e) % 4})
        found["y"].append({**here, "y": (here["y"] + e) % 4})
        other = (z + e) % 4
        found["z"].append({**here, "zh": other // 2, "zl": other % 2})
    return found


def device_of(at, core):
    return {"fsdp": at["x"] * 2 + at["zh"], "ctx": at_ctx(at["y"], at["zl"], core)}


def index_of(kept, fixed, at):
    return tuple(
        at[axis] if axis_dim in fixed else slice(None)
        for axis, axis_dim in AXES
        if axis_dim in kept
    )


def extents(kept):
    return tuple(EXTENT[axis] for axis, axis_dim in AXES if axis_dim in kept)


def span(pair):
    return pl.ds(pair[0], pair[1] - pair[0])


def cut_of(kind, part, core):
    rows, cols = CUTS[kind][part]
    at = pl.multiple_of(core * HALVES[kind] + cols[0], 128)
    return span(rows), pl.ds(at, cols[1] - cols[0])


def all_near(near, core):
    return [device_of(at, core) for dim in EVERYTHING for at in near[dim]]


class Gather:
    def __init__(self, net, outs, here, near, core):
        self.net, self.outs, self.here, self.near, self.core = net, outs, here, near, core
        self.pending, self.crossing = [[], [], []], []
        self.sibling = device_of(here, 1 - core)

    def pieces(self, part, fixed, at):
        index = index_of(EVERYTHING, fixed, at)
        return [
            ref.at[(*index, *cut_of(kind, part, self.core))] for kind, ref in self.outs.items()
        ]

    def own(self, ins, sem):
        point = index_of(EVERYTHING, EVERYTHING, self.here)
        copies = []
        for k, (kind, ref) in enumerate(self.outs.items()):
            half = HALVES[kind]
            cols = pl.ds(pl.multiple_of(self.core * half, 128), half)
            copies.append(
                pltpu.make_async_copy(
                    ins[kind].at[self.here["y"], self.here["zl"], :, cols],
                    ref.at[(*point, slice(None), cols)],
                    sem.at[k],
                )
            )
        return copies

    def stage(self, number, ins=None):
        for part, order in enumerate(ORDERS):
            steps = order[::-1]
            dim, fixed = steps[number], steps[number:]
            for copy in self.pending[part]:
                copy.wait_recv()
            refs = self.pieces(part, fixed, self.here)
            sources = refs
            if ins is not None:
                sources = [
                    ins[kind].at[
                        (self.here["y"], self.here["zl"], *cut_of(kind, part, self.core))
                    ]
                    for kind in self.outs
                ]
            self.pending[part] = [
                self.net.push(src, ref, device_of(at, self.core))
                for at in self.near[dim]
                for src, ref in zip(sources, refs)
            ]
            if number == 2:
                self.crossing += [self.net.push(ref, ref, self.sibling) for ref in refs]

    def settle(self):
        for part in range(3):
            for copy in self.pending[part]:
                copy.wait_recv()
        self.pending = [[], [], []]

    def finish(self):
        kinds = len(self.outs)
        for e in range(3):
            for part, order in enumerate(ORDERS):
                for copy in self.pending[part][kinds * e : kinds * e + kinds]:
                    copy.wait_recv()
                source = self.near[order[0]][2 - e]
                self.crossing += [
                    self.net.push(ref, ref, self.sibling)
                    for ref in self.pieces(part, (order[0],), source)
                ]
        for copy in self.crossing:
            copy.wait_recv()


def gather_shapes(kinds):
    return [
        shape_of((4, 2, 4, 2, UNIT_ROWS[kind], 2 * HALVES[kind]), jnp.bfloat16) for kind in kinds
    ]


def gather_body(in_one, small, seg, out_one, table, seg_all, got_small, own_sem, send_sem, recv_sem):
    here, core = coordinates()
    near = neighbours(here, core)
    f = here["x"] * 2 + here["zh"]
    c = at_ctx(here["y"], here["zl"], core)
    small_peers = [{"fsdp": (f + d) % FSDP} for d in range(1, FSDP)]
    meet(
        all_near(near, core)
        + [{"fsdp": (here["x"] + e) % 4 * 2 + 1 - here["zh"]} for e in range(1, 4)]
        + ctx_peers(c)
    )
    net = Sender(send_sem, recv_sem)
    gather = Gather(net, {"one": out_one}, here, near, core)
    gather.stage(0, {"one": in_one})
    own = gather.own({"one": in_one}, own_sem)
    for copy in own:
        copy.start()
    tiny = [net.push(small, got_small.at[f], peer) for peer in small_peers]
    got_small[f] = small[...]
    tiny += [net.push(seg, seg_all.at[c], peer) for peer in ctx_peers(c)]
    seg_all[c] = seg[...]
    for copy in own:
        copy.wait()
    gather.stage(1)
    gather.stage(2)
    for copy in tiny:
        copy.wait_recv()
    table[...] = jnp.zeros_like(table)
    for k in range(FSDP):
        piece = got_small[k].astype(jnp.float32)
        for first, last, width in TABLE:
            table[first:last, k * width : k * width + width] = piece[first:last, :width]
    table[9:10] = jnp.exp(table[9:10])
    table[11:12, :WIDTH] = expand(table[10:11, 0:128])
    gather.finish()
    net.drain()


TABLE = ((0, 5, 224), (5, 6, 192), (6, 8, 128), (8, 11, 3))


def gather_weights(in_one, small, seg):
    return call_kernel(
        gather_body,
        "gather_weights",
        0,
        (
            *gather_shapes(["one"]),
            shape_of((16, CONV_WIDTH), jnp.float32),
            shape_of((CTX, *seg.shape), seg.dtype),
        ),
        (in_one.reshape(4, 2, 16, COLS), small, seg),
        61,
        (pltpu.VMEM((FSDP, 16, 256), jnp.bfloat16), pltpu.SemaphoreType.DMA((2,))),
        (0,),
        (0,),
    )


def ctx_peers(c):
    return [{"ctx": (c + e) % CTX} for e in range(1, CTX)]


def expand(per_head):
    rows = per_head.shape[0]
    lane = lax.broadcasted_iota(jnp.int32, (rows, 128), 1)
    return jnp.concatenate(
        [
            jnp.where(
                lane < SSM_DIM,
                jnp.broadcast_to(per_head[:, 2 * j : 2 * j + 1], (rows, 128)),
                jnp.broadcast_to(per_head[:, 2 * j + 1 : 2 * j + 2], (rows, 128)),
            )
            for j in range(SSM_HEADS // 2)
        ],
        axis=1,
    )


def pack(states, chunks):
    for k in range(CTX):
        rows = states[8 * k : 8 * k + 8]
        chunks[k] = jnp.concatenate([rows[:, :HALF_WIDTH], rows[:, HALF_WIDTH:]], axis=0).astype(
            jnp.bfloat16
        )


def unpack(chunks, states):
    for k in range(CTX):
        rows = chunks[k].astype(jnp.float32)
        states[8 * k : 8 * k + 8] = jnp.concatenate([rows[:8], rows[8:]], axis=1)


def scan_rows(order, decay_of, parts, carries):
    wide = expand(jnp.concatenate([decay_of[k, 0:1] for k in range(CTX)], axis=0))
    state = jnp.zeros((16, HALF_WIDTH), jnp.float32)
    for at in order:
        carries[at] = state.astype(jnp.bfloat16)
        decay = jnp.concatenate(
            [
                jnp.broadcast_to(wide[at : at + 1, :HALF_WIDTH], (8, HALF_WIDTH)),
                jnp.broadcast_to(wide[at : at + 1, HALF_WIDTH:], (8, HALF_WIDTH)),
            ],
            axis=0,
        )
        state = decay * state + parts[at].astype(jnp.float32)


def send_back(net, c, peers, carries, carried):
    copies = [
        net.push(carries.at[(c + e + 1) % CTX], carried.at[c], peer) for e, peer in enumerate(peers)
    ]
    carried[c] = carries[c]
    return copies


def across(left, right):
    return lax.dot_general(
        left, right, (((1,), (1,)), ((), ())), preferred_element_type=jnp.float32
    )


def down(left, right):
    return lax.dot_general(
        left, right, (((0,), (0,)), ((), ())), preferred_element_type=jnp.float32
    )


def forward_body(
    query,
    kv,
    hidden_mask,
    inner,
    steps,
    masks,
    intra,
    table,
    in_two,
    in_three,
    kv_all,
    rim_all,
    mixed,
    cumulative,
    sizes,
    entering,
    carried,
    result,
    decays,
    attended,
    log_total,
    out_two,
    out_three,
    states,
    inside,
    extended,
    wide_states,
    parts,
    carries,
    came_back,
    decay,
    own_sem,
    send_sem,
    recv_sem,
):
    here, core = coordinates()
    near = neighbours(here, core)
    c = at_ctx(here["y"], here["zl"], core)
    peers = ctx_peers(c)
    rows = kv_all.shape[1]
    meet(peers + all_near(near, core))
    net = Sender(send_sem, recv_sem)
    rim_copy = net.push(inner.at[pl.ds(rows - 8, 8)], rim_all, peers[0])
    key_copies = [net.push(kv, kv_all.at[c], peer) for peer in peers]
    ins = {"two": in_two, "three": in_three}
    gather = Gather(net, {"two": out_two, "three": out_three}, here, near, core)
    gather.stage(0, ins)
    own = gather.own(ins, own_sem)
    for copy in own:
        copy.start()
    kv_all[c] = kv[...]
    for copy in own:
        copy.wait()
    gather.stage(1)
    rim_copy.wait_recv()
    mixer_parts_body(
        inner,
        rim_all,
        steps,
        masks,
        intra,
        table,
        mixed,
        cumulative,
        sizes,
        states,
        decay,
        entering,
        inside,
        extended,
        wide_states,
    )
    copies = []
    for e, peer in enumerate(peers):
        copies.append(net.push(states.at[(c + e + 1) % CTX], parts.at[c], peer))
        copies.append(net.push(decay, decays.at[c], peer))
    parts[c] = states[c]
    decays[c] = decay[...]
    gather.stage(2)
    for copy in key_copies:
        copy.wait_recv()

    def head(h, nothing):
        keys = kv_all[:, :, 0:128].reshape(CTX * rows, 128)
        values = kv_all[:, :, 128:256].reshape(CTX * rows, 128)
        scores = across(query[h], keys) + hidden_mask[...]
        row_max = jnp.max(scores, axis=-1, keepdims=True)
        weights = jnp.exp(scores - row_max)
        row_sum = jnp.sum(weights, axis=-1, keepdims=True)
        probs = (weights * (1.0 / row_sum)).astype(jnp.bfloat16)
        attended[h] = jnp.dot(probs, values, preferred_element_type=jnp.float32).astype(
            jnp.bfloat16
        )
        log_total[h] = jnp.broadcast_to(row_max + jnp.log(row_sum), (rows, 128))
        return nothing

    lax.fori_loop(0, 3, head, 0)
    for copy in copies:
        copy.wait_recv()
    scan_rows(range(CTX), decays, parts, carries)
    back = send_back(net, c, peers, carries, came_back)
    lax.fori_loop(3, HEADS, head, 0)
    for copy in back:
        copy.wait_recv()
    unpack(came_back, carried)
    output_map = mixed[:, WIDTH + STATE :].astype(jnp.bfloat16)
    result[...] = inside[...] + expand(entering[...]) * jnp.dot(
        output_map, carried[...].astype(jnp.bfloat16), preferred_element_type=jnp.float32
    )
    gather.finish()
    net.drain()


def forward(query, kv, hidden_mask, inner, steps, masks, intra, table, two, three):
    rows = query.shape[1]
    f32, low = jnp.float32, jnp.bfloat16
    return call_kernel(
        forward_body,
        "forward",
        1,
        (
            shape_of((CTX, *kv.shape), kv.dtype),
            shape_of((8, CONV_WIDTH), f32),
            shape_of((rows, CONV_WIDTH), f32),
            shape_of((rows, 128), f32),
            shape_of((rows, 128), f32),
            shape_of((rows, 128), f32),
            shape_of((STATE, WIDTH), f32),
            shape_of((rows, WIDTH), f32),
            shape_of((CTX, 8, 128), f32),
            shape_of((HEADS, rows, 128), low),
            shape_of((HEADS, rows, 128), f32),
            *gather_shapes(["two", "three"]),
        ),
        (
            query,
            kv,
            hidden_mask,
            inner,
            steps,
            masks,
            intra,
            table,
            two.reshape(4, 2, 16, 2 * HALVES["two"]),
            three.reshape(4, 2, 64, 2 * HALVES["three"]),
        ),
        139,
        (
            pltpu.VMEM((CTX, 16, HALF_WIDTH), low),
            pltpu.VMEM((rows, WIDTH), f32),
            pltpu.VMEM((rows + 8, CONV_WIDTH), f32),
            pltpu.VMEM((STATE, WIDTH), f32),
            *[pltpu.VMEM((CTX, 16, HALF_WIDTH), low)] * 3,
            pltpu.VMEM((8, 128), f32),
            pltpu.SemaphoreType.DMA((2,)),
        ),
        (8, 9),
        (11, 12),
    )


def plain_kernel(body, name, outs, ins, scratch=()):
    return pl.pallas_call(
        body,
        name=name,
        out_shape=outs,
        in_specs=[pl.BlockSpec(memory_space=pltpu.VMEM)] * len(ins),
        out_specs=tuple(pl.BlockSpec(memory_space=pltpu.VMEM) for _ in outs),
        scratch_shapes=list(scratch),
        compiler_params=pltpu.CompilerParams(vmem_limit_bytes=VMEM_LIMIT),
    )(*ins)


TAP_ROWS = 8 - CONV + 1


def conv_sum(extended, masks, conv_par, at):
    rows = masks.shape[0]
    total = jnp.broadcast_to(conv_par[CONV : CONV + 1, at], (rows, conv_par[0:1, at].shape[1]))
    for tap in range(CONV):
        first = TAP_ROWS + tap
        term = conv_par[tap : tap + 1, at] * extended[first : first + rows, at]
        total = total + (term * masks[:, tap : tap + 1] if tap < CONV - 1 else term)
    return total


def lower_ones(rows):
    at = lax.broadcasted_iota(jnp.int32, (rows, rows), 0)
    return (at >= lax.broadcasted_iota(jnp.int32, (rows, rows), 1)).astype(jnp.float32)


def exact(left, right, contract):
    return lax.dot_general(
        left,
        right,
        ((contract[0], contract[1]), ((), ())),
        precision=highest,
        preferred_element_type=jnp.float32,
    )


def swap_quarters(values):
    lane = lax.broadcasted_iota(jnp.int32, values.shape, 1)
    quarter = HEAD_DIM // 2
    ahead = jnp.concatenate([values[:, quarter:], values[:, :quarter]], axis=1)
    behind = jnp.concatenate([values[:, 128 - quarter :], values[:, : 128 - quarter]], axis=1)
    return jnp.where(lane % HEAD_DIM < quarter, ahead, behind)


def split_pair(both, j, out):
    lane = lax.broadcasted_iota(jnp.int32, both.shape, 1)
    turned = shift_half(both)
    low = jnp.bfloat16
    if j < HEADS // 4:
        out[2 * j] = jnp.where(lane < HEAD_DIM, both, 0.0).astype(low)
        out[2 * j + 1] = jnp.where(lane < HEAD_DIM, turned, 0.0).astype(low)
    else:
        out[2 * j] = jnp.where(lane < HEAD_DIM, 0.0, turned).astype(low)
        out[2 * j + 1] = jnp.where(lane < HEAD_DIM, 0.0, both).astype(low)


def join_pair(values, j):
    first, second = values[2 * j].astype(jnp.float32), values[2 * j + 1].astype(jnp.float32)
    if j < HEADS // 4:
        second = shift_half(second)
    else:
        first = shift_half(first)
    lane = lax.broadcasted_iota(jnp.int32, first.shape, 1)
    return jnp.where(lane < HEAD_DIM, first, second)


Z_AT = HEADS * HEAD_DIM + 2 * KV_HEADS * HEAD_DIM
INNER_AT = Z_AT + WIDTH
STEP_AT = INNER_AT + CONV_WIDTH


def project_body(row_in, table, cosine, sine, weights, norm_low, query, kv, gate_z, inner, steps):
    values = row_in[...]
    scale = lax.rsqrt(mean_last(values * values) + epsilon)
    normed = (values * scale * table[7:8, 0 : values.shape[1]]).astype(jnp.bfloat16)
    norm_low[...] = normed

    def part(first, last):
        return jnp.dot(normed, weights[:, first:last], preferred_element_type=jnp.float32)

    def turn(both):
        return both * cosine[...] + swap_quarters(both) * sine[...]

    for j in range(HEADS // 2):
        split_pair(turn(part(128 * j, 128 * j + 128)) * HEAD_DIM ** (-0.5), j, query)
    key_at = HEADS * HEAD_DIM
    kv[:, 0:128] = (turn(part(key_at, key_at + 128)) * key_scale).astype(jnp.bfloat16)
    kv[:, 128:256] = part(key_at + 128, key_at + 256).astype(jnp.bfloat16)
    for at in range(0, WIDTH, 512):
        gate_z[:, at : at + 512] = part(Z_AT + at, Z_AT + at + 512)
    for at in range(0, CONV_WIDTH, 256):
        inner[:, at : at + 256] = part(INNER_AT + at, INNER_AT + at + 256)
    steps[...] = part(STEP_AT, STEP_AT + 128)


def project(row_in, table, cosine, sine, weights):
    rows, dim = row_in.shape
    f32, low = jnp.float32, jnp.bfloat16
    return plain_kernel(
        project_body,
        "project",
        (
            shape_of((rows, dim), low),
            shape_of((HEADS, rows, 128), low),
            shape_of((rows, 256), low),
            shape_of((rows, WIDTH), f32),
            shape_of((rows, CONV_WIDTH), f32),
            shape_of((rows, 128), f32),
        ),
        (row_in, table, cosine, sine, weights),
    )


def mixer_parts_body(
    inner,
    rim,
    steps,
    masks,
    intra,
    table,
    mixed,
    cumulative,
    sizes,
    chunks,
    decay,
    entering,
    inside,
    extended,
    states,
):
    rows = inner.shape[0]
    low = jnp.bfloat16
    extended[0:8] = rim[...]
    extended[8:] = inner[...]
    for piece in range(CONV_WIDTH // 256):
        at = slice(piece * 256, piece * 256 + 256)
        total = conv_sum(extended, masks, table, at)
        mixed[:, at] = total / (1.0 + jnp.exp(-total))
    raw = steps[...] + table[8:9, 0:128]
    size = jnp.maximum(raw, 0.0) + jnp.log1p(jnp.exp(-jnp.abs(raw)))
    sums = exact(lower_ones(rows), -size * table[9:10, 0:128], ((1,), (0,)))
    cumulative[...] = sums
    sizes[...] = size
    last = sums[rows - 1 : rows]
    entering[...] = jnp.exp(sums) * masks[:, 3:4]
    decay[...] = jnp.broadcast_to(jnp.exp(last) * masks[0:1, 5:6], (8, 128))
    tail = masks[:, 4:5] * jnp.exp(last - sums) * size
    weighted = (expand(tail) * mixed[:, :WIDTH]).astype(low)
    input_map = mixed[:, WIDTH : WIDTH + STATE]
    output_map = mixed[:, WIDTH + STATE :]
    states[...] = down(input_map.astype(low), weighted)
    pack(states, chunks)
    pairing = exact(output_map, input_map, ((1,), (1,))) * intra[...]
    sums_t, size_t = sums.T, size.T
    lane = lax.broadcasted_iota(jnp.int32, (rows, 128), 1)
    for j in range(SSM_HEADS // 2):
        at = slice(128 * j, 128 * j + 128)
        values = mixed[:, at]
        found = []
        for h in (2 * j, 2 * j + 1):
            spread = jnp.minimum(sums[:, h : h + 1] - sums_t[h : h + 1], 0.0)
            mixing = (jnp.exp(spread) * pairing * size_t[h : h + 1]).astype(low)
            found.append(jnp.dot(mixing, values.astype(low), preferred_element_type=jnp.float32))
        inside[:, at] = jnp.where(lane < SSM_DIM, found[0], found[1]) + table[11:12, at] * values


def mean_last(values):
    return jnp.mean(values, axis=-1, keepdims=True)


def pair_of(weights, j, first, last):
    return jnp.concatenate([weights[2 * j, first:last], weights[2 * j + 1, first:last]], axis=0)


def shift_half(values):
    return jnp.concatenate([values[:, HEAD_DIM:], values[:, :HEAD_DIM]], axis=1)


def middle_body(
    row_in,
    row_grad,
    attended,
    result,
    gate_z,
    table,
    w_two,
    w_three,
    row_out,
    grad_middle,
    attn_low,
    mixer_low,
    hidden_low,
    norm_low,
    grads_two,
    grads_three,
    grad_out,
    grad_result,
    grad_z,
    grad_ffn_gain,
    grad_mixer_gain,
    down_sum,
    norm_sum,
    grad_flat,
):
    low, f32 = jnp.bfloat16, jnp.float32
    attn_sum = jnp.zeros(row_in.shape, f32)
    for j in range(HEADS // 2):
        both = join_pair(attended, j).astype(low)
        attn_low[:, 128 * j : 128 * j + 128] = both
        attn_sum = attn_sum + jnp.dot(
            both, pair_of(w_three, j, 0, 64), preferred_element_type=f32
        )
    z, mixed_out = gate_z[...], result[...]
    sig_z = 1.0 / (1.0 + jnp.exp(-z))
    flat = mixed_out * (z * sig_z)
    scale = lax.rsqrt(mean_last(flat * flat) + epsilon)
    normed = (flat * scale * table[5:6, 0:WIDTH]).astype(low)
    mixer_low[...] = normed
    mixer_sum = jnp.zeros(row_in.shape, f32)
    for j in range(4):
        mixer_sum = mixer_sum + jnp.dot(
            normed[:, 384 * j : 384 * j + 384],
            pair_of(w_three, j, 64, 256),
            preferred_element_type=f32,
        )
    middle = row_in[...] + attn_sum * attn_out_scale + mixer_sum * mixer_out_scale
    scale_two = lax.rsqrt(mean_last(middle * middle) + epsilon)
    norm_low[...] = (middle * scale_two * table[6:7, 0 : row_in.shape[1]]).astype(low)
    grad_down = (row_grad[...] * down_scale).astype(low)
    grads_three[2] = grad_down
    down_sum[...] = jnp.zeros_like(down_sum)
    norm_sum[...] = jnp.zeros_like(norm_sum)
    ff_width = FSDP * 256

    def chunk(f, nothing):
        at = pl.ds(pl.multiple_of(f * 256, 256), 256)
        at_up = pl.ds(pl.multiple_of(ff_width + f * 256, 256), 256)
        w_gate, w_up, w_down = w_two[:, at], w_two[:, at_up], w_three[f, 256:512]
        gate = jnp.dot(norm_low[...], w_gate, preferred_element_type=f32) * gate_scale
        up = jnp.dot(norm_low[...], w_up, preferred_element_type=f32)
        sig = 1.0 / (1.0 + jnp.exp(-gate))
        hidden = (gate * sig * up).astype(low)
        hidden_low[:, at] = hidden
        down_sum[...] += jnp.dot(hidden, w_down, preferred_element_type=f32)
        grad_hidden = across(grad_down, w_down)
        grad_gate = (
            grad_hidden * up * sig * (1.0 + gate * (1.0 - sig)) * gate_scale
        ).astype(low)
        grad_up = (grad_hidden * gate * sig).astype(low)
        grads_two[:, at] = grad_gate
        grads_two[:, at_up] = grad_up
        norm_sum[...] += across(grad_gate, w_gate) + across(grad_up, w_up)
        return nothing

    lax.fori_loop(0, FSDP, chunk, 0)
    row_out[...] = (middle + down_sum[...] * down_scale).astype(low)
    grad_norm = norm_sum[...]
    weighted = grad_norm * table[6:7, 0 : row_in.shape[1]]
    grad_mid = (
        row_grad[...]
        + scale_two * weighted
        - middle * (scale_two * scale_two * scale_two) * mean_last(middle * weighted)
    )
    grad_middle[...] = grad_mid
    grad_ffn_gain[...] = jnp.broadcast_to(
        jnp.sum(grad_norm * middle * scale_two, axis=0, keepdims=True), grad_ffn_gain.shape
    )
    grad_attn = (grad_mid * attn_out_scale).astype(low)
    grad_mix = (grad_mid * mixer_out_scale).astype(low)
    grads_three[0] = grad_attn
    grads_three[1] = grad_mix
    for j in range(HEADS // 2):
        split_pair(across(grad_attn, pair_of(w_three, j, 0, 64)), j, grad_out)
    for j in range(4):
        grad_flat[:, 384 * j : 384 * j + 384] = across(grad_mix, pair_of(w_three, j, 64, 256))
    grad_normed = grad_flat[...]
    weighted = grad_normed * table[5:6, 0:WIDTH]
    grad_mixer_gain[...] = jnp.broadcast_to(
        jnp.sum(grad_normed * flat * scale, axis=0, keepdims=True), grad_mixer_gain.shape
    )
    grad_gated = scale * weighted - flat * (scale * scale * scale) * mean_last(flat * weighted)
    grad_result[...] = grad_gated * (z * sig_z)
    grad_z[...] = (grad_gated * mixed_out * sig_z * (1.0 + z * (1.0 - sig_z))).astype(low)


def middle_part(row_in, row_grad, attended, result, gate_z, table, w_two, w_three):
    rows, dim = row_in.shape
    f32, low = jnp.float32, jnp.bfloat16
    return plain_kernel(
        middle_body,
        "middle_part",
        (
            shape_of((rows, dim), low),
            shape_of((rows, dim), f32),
            shape_of((rows, HEADS * HEAD_DIM), low),
            shape_of((rows, WIDTH), low),
            shape_of((rows, FSDP * 256), low),
            shape_of((rows, dim), low),
            shape_of((rows, 2 * FSDP * 256), low),
            shape_of((3, rows, dim), low),
            shape_of((HEADS, rows, 128), low),
            shape_of((rows, WIDTH), f32),
            shape_of((rows, WIDTH), low),
            shape_of((8, dim), f32),
            shape_of((8, WIDTH), f32),
        ),
        (row_in, row_grad, attended, result, gate_z, table, w_two, w_three),
        (
            pltpu.VMEM((rows, dim), f32),
            pltpu.VMEM((rows, dim), f32),
            pltpu.VMEM((rows, WIDTH), f32),
        ),
    )


def mixer_grads_body(
    grad,
    leaving,
    carried,
    mixed,
    cumulative,
    sizes,
    entering,
    inner,
    rim,
    steps,
    masks,
    intra,
    table,
    grad_inner,
    grad_rim,
    grad_steps,
    grad_conv,
    grad_heads,
    extended,
    grad_ext,
    grad_mixed,
):
    rows = inner.shape[0]
    low = jnp.bfloat16
    sums, size = cumulative[...], sizes[...]
    last = sums[rows - 1 : rows]
    input_map = mixed[:, WIDTH : WIDTH + STATE]
    output_map = mixed[:, WIDTH + STATE :]
    gather_head = (
        lax.broadcasted_iota(jnp.int32, (WIDTH, 128), 0) // SSM_DIM
        == lax.broadcasted_iota(jnp.int32, (WIDTH, 128), 1)
    ).astype(jnp.float32)

    def per_head(wide):
        return exact(wide, gather_head, ((1,), (0,)))

    tail_decay = masks[:, 4:5] * jnp.exp(last - sums)
    tail = tail_decay * size
    leaving_low, carried_low = leaving[...].astype(low), carried[...].astype(low)
    from_state = jnp.dot(input_map.astype(low), leaving_low, preferred_element_type=jnp.float32)
    to_output = jnp.dot(output_map.astype(low), carried_low, preferred_element_type=jnp.float32)
    wide_tail = expand(tail)
    values_all, grad_all = mixed[:, :WIDTH], grad[...]
    grad_tail = per_head(values_all * from_state)
    grad_entering = per_head(grad_all * to_output)
    grad_skip = per_head(jnp.sum(grad_all * values_all, axis=0, keepdims=True))
    grad_block = per_head(jnp.sum(leaving[...] * carried[...], axis=0, keepdims=True))
    grad_input = across((wide_tail * values_all).astype(low), leaving_low)
    grad_output = across((expand(entering[...]) * grad_all).astype(low), carried_low)
    grad_mixed[:, :WIDTH] = wide_tail * from_state + table[11:12, 0:WIDTH] * grad_all

    pairing = exact(output_map, input_map, ((1,), (1,)))
    sums_t, size_t = sums.T, size.T
    lane = lax.broadcasted_iota(jnp.int32, (rows, 128), 1)
    grad_pairing = jnp.zeros((rows, rows), jnp.float32)
    row_sums = jnp.zeros((rows, 128), jnp.float32)
    size_rows = []
    for j in range(SSM_HEADS // 2):
        at = slice(128 * j, 128 * j + 128)
        values, grads = mixed[:, at].astype(low), grad[:, at]
        found = []
        for h in (2 * j, 2 * j + 1):
            own_lanes = lane < SSM_DIM if h == 2 * j else lane >= SSM_DIM
            spread = jnp.minimum(sums[:, h : h + 1] - sums_t[h : h + 1], 0.0)
            decays = jnp.exp(spread) * intra[...]
            inner_part = decays * pairing
            mixing = inner_part * size_t[h : h + 1]
            found.append(down(mixing.astype(low), grads.astype(low)))
            grad_mixing = across(jnp.where(own_lanes, grads, 0.0).astype(low), values)
            grad_pairing = grad_pairing + grad_mixing * decays * size_t[h : h + 1]
            by_size = grad_mixing * inner_part
            size_rows.append(jnp.sum(by_size, axis=0, keepdims=True))
            row_sum = jnp.sum(by_size * size_t[h : h + 1], axis=1, keepdims=True)
            row_sums = jnp.where(lane == h, row_sum, row_sums)
        grad_mixed[:, at] += jnp.where(lane < SSM_DIM, found[0], found[1])
    size_rows.append(jnp.zeros((128 - SSM_HEADS, rows), jnp.float32))
    grad_size = jnp.concatenate(size_rows, axis=0).T
    grad_sums = row_sums - size * grad_size
    grad_size = grad_size + grad_tail * tail_decay
    by_tail = grad_tail * tail
    grad_sums = grad_sums - by_tail + grad_entering * entering[...]
    grad_last = jnp.sum(by_tail, axis=0, keepdims=True) + grad_block * (
        jnp.exp(last) * masks[0:1, 5:6]
    )
    row = lax.broadcasted_iota(jnp.int32, (rows, 128), 0)
    grad_sums = grad_sums + jnp.where(row == rows - 1, grad_last, 0.0)
    grad_log = exact(lower_ones(rows), grad_sums, ((0,), (0,)))
    rate = table[9:10, 0:128]
    grad_size = grad_size - rate * grad_log
    raw = steps[...] + table[8:9, 0:128]
    grad_raw = grad_size / (1.0 + jnp.exp(-raw))
    grad_steps[...] = grad_raw
    grad_heads[...] = jnp.concatenate(
        [
            jnp.sum(grad_raw, axis=0, keepdims=True),
            jnp.sum(-grad_log * size * rate, axis=0, keepdims=True),
            grad_skip,
            jnp.zeros((5, 128), jnp.float32),
        ],
        axis=0,
    )
    grad_pairing = grad_pairing.astype(low)
    grad_mixed[:, WIDTH : WIDTH + STATE] = grad_input + down(grad_pairing, output_map.astype(low))
    grad_mixed[:, WIDTH + STATE :] = grad_output + jnp.dot(
        grad_pairing, input_map.astype(low), preferred_element_type=jnp.float32
    )

    extended[0:8] = rim[...]
    extended[8:] = inner[...]
    grad_ext[...] = jnp.zeros_like(grad_ext)
    for piece in range(CONV_WIDTH // 256):
        at = slice(piece * 256, piece * 256 + 256)
        total = conv_sum(extended, masks, table, at)
        sig = 1.0 / (1.0 + jnp.exp(-total))
        grad_total = grad_mixed[:, at] * sig * (1.0 + total * (1.0 - sig))
        taps = []
        for tap in range(CONV):
            first = TAP_ROWS + tap
            kept = grad_total * masks[:, tap : tap + 1] if tap < CONV - 1 else grad_total
            taps.append(jnp.sum(kept * extended[first : first + rows, at], axis=0, keepdims=True))
            grad_ext[first : first + rows, at] += table[tap : tap + 1, at] * kept
        taps.append(jnp.sum(grad_total, axis=0, keepdims=True))
        taps.append(jnp.zeros((8 - CONV - 1, 256), jnp.float32))
        grad_conv[:, at] = jnp.concatenate(taps, axis=0)
    grad_rim[...] = grad_ext[0:8]
    grad_inner[...] = grad_ext[8:]


def dot_rows(left, right):
    return down(left, right).astype(jnp.bfloat16)


class Sums:
    def __init__(self, net, kinds, here, near, core, came, summed, own=None):
        self.net, self.kinds, self.here, self.near, self.core = net, kinds, here, near, core
        self.came, self.summed, self.own = came, summed, own
        self.pending = [None, None, None]

    def refs(self, part, stage, fixed, at):
        index = index_of(ORDERS[part][stage:], fixed, at)
        if stage:
            return [ref.at[index] for ref in self.summed[part, stage - 1]]
        return [
            ref.at[(*index, *(span(pair) for pair in CUTS[kind][part]))]
            for kind, ref in zip(self.kinds, self.own)
        ]

    def early(self, e, send_sem, recv_sem):
        at = {**self.here, "x": (self.here["x"] + e + 1) % 4}
        return [
            pltpu.make_async_remote_copy(
                src_ref=src,
                dst_ref=dst.at[e],
                send_sem=send_sem.at[len(self.kinds) * e + k],
                recv_sem=recv_sem.at[len(self.kinds) * e + k],
                device_id=device_of(at, self.core),
                device_id_type=MESH,
            )
            for k, (src, dst) in enumerate(
                zip(self.refs(0, 0, ("x",), at), self.came[0, 0])
            )
        ]

    def send(self, part, stage):
        dim = ORDERS[part][stage]
        self.pending[part] = [
            self.net.push(src, dst.at[e], device_of(at, self.core))
            for e, at in enumerate(self.near[dim])
            for src, dst in zip(self.refs(part, stage, (dim,), at), self.came[part, stage])
        ]

    def wait(self, part):
        for copy in self.pending[part] or ():
            copy.wait_recv()

    def add_up(self, part, stage):
        kept, rest = ORDERS[part][stage:], ORDERS[part][stage + 1 :]

        def unit(number, nothing):
            at, left = dict(self.here), number
            for axis, axis_dim in reversed(AXES):
                if axis_dim in rest:
                    at[axis] = left % EXTENT[axis]
                    left = left // EXTENT[axis]
            inner = index_of(rest, rest, at)
            own_refs = self.refs(part, stage, kept, at)
            for own, came, out in zip(
                own_refs, self.came[part, stage], self.summed[part, stage]
            ):
                total = own[...].astype(jnp.float32)
                for e in range(3):
                    total = total + came[(e, *inner)].astype(jnp.float32)
                out[inner if inner else Ellipsis] = total.astype(jnp.bfloat16)
            return nothing

        count = 1
        for size in extents(rest):
            count *= size
        if count == 1:
            unit(0, 0)
        else:
            lax.fori_loop(0, count, unit, 0)


def piece_shapes(kinds, part):
    return [
        tuple(pair[1] - pair[0] for pair in CUTS[kind][part]) for kind in kinds
    ]


def came_shapes(kinds, part, stage):
    rest = extents(ORDERS[part][stage + 1 :])
    return [(3, *rest, *shape) for shape in piece_shapes(kinds, part)]


def summed_shapes(kinds, part, stage):
    rest = extents(ORDERS[part][stage + 1 :])
    return [(*rest, *shape) for shape in piece_shapes(kinds, part)]


def stage_keys(stages):
    return [(part, stage) for part in range(3) for stage in stages]


def take(refs, keys, kinds):
    found = {}
    for key in keys:
        found[key], refs = refs[: len(kinds)], refs[len(kinds) :]
    return found, refs


def low_scratch(shapes):
    return [pltpu.VMEM(dims, jnp.bfloat16) for dims in shapes]


def half_of(core, kind):
    return pl.ds(pl.multiple_of(core * HALVES[kind], 128), HALVES[kind])


LATE = ("two", "three")


def backward_body(
    grad,
    mixed,
    entering,
    decays,
    query,
    grad_out,
    kv_all,
    hidden_mask,
    log_total,
    norm,
    grads_two,
    acts_attn,
    acts_mixer,
    acts_hidden,
    grads_three,
    carried,
    cumulative,
    sizes,
    inner,
    rim,
    steps,
    masks,
    intra,
    table,
    cosine,
    sine,
    grad_z,
    grads_one,
    grad_conv,
    grad_heads,
    out_two,
    out_three,
    *rest,
):
    came, rest = take(rest, stage_keys(range(3)), LATE)
    summed, rest = take(rest, stage_keys(range(3)), LATE)
    states, parts, carries, came_back, terms, term_parts = rest[:6]
    both_norm, both_two, both_act, both_three, own_two, own_three = rest[6:12]
    key_sum, value_sum, wide_states, leaving, grad_query, grad_inner, grad_rim, rim_back = rest[12:20]
    extended, grad_ext, grad_mixed, grad_steps, send_sem, recv_sem = rest[20:]
    here, core = coordinates()
    near = neighbours(here, core)
    c = at_ctx(here["y"], here["zl"], core)
    peers = ctx_peers(c)
    meet(peers + all_near(near, core))
    net = Sender(send_sem.at[pl.ds(6, 100)], recv_sem.at[pl.ds(6, 100)])
    sibling = device_of(here, 1 - core)
    toks = norm.shape[0]
    mine, theirs = pl.ds(0, toks), pl.ds(toks, toks)
    other = 1 - core
    first = [
        net.push(norm, both_norm.at[theirs], sibling),
        net.push(grads_two.at[:, half_of(other, "two")], both_two.at[theirs], sibling),
        net.push(acts_attn, both_act.at[theirs, pl.ds(0, 512)], sibling),
        net.push(acts_mixer, both_act.at[theirs, pl.ds(512, 1536)], sibling),
        net.push(acts_hidden, both_act.at[theirs, pl.ds(2048, 2048)], sibling),
        net.push(grads_three.at[:, :, half_of(other, "three")], both_three.at[:, theirs], sibling),
    ]
    both_norm[mine] = norm[...]
    both_two[mine] = grads_two[:, half_of(core, "two")]
    both_act[mine, 0:512] = acts_attn[...]
    both_act[mine, 512:2048] = acts_mixer[...]
    both_act[mine, 2048:4096] = acts_hidden[...]
    both_three[:, mine] = grads_three[:, :, half_of(core, "three")]
    output_map = mixed[:, WIDTH + STATE :].astype(jnp.bfloat16)
    wide_states[...] = down(
        output_map, (expand(entering[...]) * grad[...]).astype(jnp.bfloat16)
    )
    pack(wide_states, states)
    copies = [
        net.push(states.at[(c + e + 1) % CTX], parts.at[c], peer) for e, peer in enumerate(peers)
    ]
    parts[c] = states[c]
    for copy in first:
        copy.wait_recv()

    def block(owner_x):
        features = both_norm[:, pl.ds(pl.multiple_of(owner_x * 256, 256), 256)]
        wide = HALVES["two"] // 2
        for piece in range(2):
            at = pl.ds(piece * wide, wide)
            found = dot_rows(features, both_two[:, at])
            for unit in range(16):
                own_two[owner_x, unit // 8, unit // 2 % 4, unit % 2, :, at] = found[
                    unit * 16 : unit * 16 + 16
                ]
        found = []
        for source, (start, size) in enumerate(((0, 128), (512, 384), (2048, 512))):
            at = pl.ds(pl.multiple_of(start + owner_x * size, 128), size)
            found.append(dot_rows(both_act[:, at], both_three[source]))
        for owner_z in range(2):
            for unit in range(8):
                source = 0 if unit < 1 else 1 if unit < 4 else 2
                at = (unit - (0, 1, 4)[source]) * 64 + owner_z * (64, 192, 256)[source]
                own_three[owner_x, owner_z, unit // 2, unit % 2] = found[source][at : at + 64]

    sums = Sums(net, LATE, here, near, core, came, summed, (own_two, own_three))

    def turn(e, nothing):
        block((here["x"] + e + 1) % 4)
        for copy in sums.early(e, send_sem, recv_sem):
            copy.start()
        return nothing

    lax.fori_loop(0, 3, turn, 0)
    block(here["x"])
    sums.send(1, 0)
    sums.send(2, 0)
    for copy in copies:
        copy.wait_recv()
    scan_rows(range(CTX - 1, -1, -1), decays, parts, carries)
    back = send_back(net, c, peers, carries, came_back)
    key_sum[...] = jnp.zeros_like(key_sum)
    value_sum[...] = jnp.zeros_like(value_sum)

    def head(h, nothing):
        keys = kv_all[:, :, 0:128].reshape(CTX * toks, 128)
        values = kv_all[:, :, 128:256].reshape(CTX * toks, 128)
        scores = across(query[h], keys) + hidden_mask[...]
        probs = jnp.exp(scores - log_total[h][:, 0:1])
        grad_probs = across(grad_out[h], values)
        inner_sum = jnp.sum(probs * grad_probs, axis=-1, keepdims=True)
        grad_scores = (probs * (grad_probs - inner_sum)).astype(jnp.bfloat16)
        grad_query[h] = jnp.dot(grad_scores, keys, preferred_element_type=jnp.float32)
        key_sum[...] += down(query[h], grad_scores)
        value_sum[...] += down(grad_out[h], probs.astype(jnp.bfloat16))
        return nothing

    lax.fori_loop(0, HEADS, head, 0)
    for k in range(CTX):
        at = pl.ds(k * toks, toks)
        terms[k, 0:128] = key_sum[:, at].astype(jnp.bfloat16)
        terms[k, 128:256] = value_sum[:, at].astype(jnp.bfloat16)
    key_copies = [
        net.push(terms.at[(c + e + 1) % CTX], term_parts.at[e], peer)
        for e, peer in enumerate(peers)
    ]
    for copy in back:
        copy.wait_recv()
    unpack(came_back, leaving)
    mixer_grads_body(
        grad,
        leaving,
        carried,
        mixed,
        cumulative,
        sizes,
        entering,
        inner,
        rim,
        steps,
        masks,
        intra,
        table,
        grad_inner,
        grad_rim,
        grad_steps,
        grad_conv,
        grad_heads,
        extended,
        grad_ext,
        grad_mixed,
    )
    rim_copy = net.push(grad_rim, rim_back, peers[-1])
    for e in range(3):
        for copy in sums.early(e, send_sem, recv_sem):
            copy.wait_recv()
    for part in range(3):
        sums.wait(part)
        sums.add_up(part, 0)
        sums.send(part, 1)

    def turn_back(both):
        return both * cosine[...] - swap_quarters(both) * sine[...]

    low = jnp.bfloat16
    for j in range(HEADS // 2):
        grads_one[:, 128 * j : 128 * j + 128] = (
            turn_back(join_pair(grad_query, j)) * HEAD_DIM ** (-0.5)
        ).astype(low)
    for copy in key_copies:
        copy.wait_recv()
    collected = terms[c].astype(jnp.float32)
    for e in range(CTX - 1):
        collected = collected + term_parts[e].astype(jnp.float32)
    key_at = HEADS * HEAD_DIM
    grads_one[:, key_at : key_at + 128] = (turn_back(collected[0:128].T) * key_scale).astype(low)
    grads_one[:, key_at + 128 : Z_AT] = collected[128:256].T.astype(low)
    grads_one[:, Z_AT:INNER_AT] = grad_z[...]
    rim_copy.wait_recv()
    grad_inner[toks - 8 :] = grad_inner[toks - 8 :] + rim_back[...]
    grads_one[:, INNER_AT:STEP_AT] = grad_inner[...].astype(low)
    grads_one[:, STEP_AT : STEP_AT + 128] = grad_steps[...].astype(low)
    grads_one[:, PAD_AT:COLS] = jnp.zeros((toks, COLS - PAD_AT), low)
    for part in range(3):
        sums.wait(part)
        sums.add_up(part, 1)
        sums.send(part, 2)
    for part in range(3):
        sums.wait(part)
        sums.add_up(part, 2)
        for kind, out, ref in zip(LATE, (out_two, out_three), summed[part, 2]):
            out[tuple(span(pair) for pair in CUTS[kind][part])] = ref[...]
    for e in range(3):
        for copy in sums.early(e, send_sem, recv_sem):
            copy.wait_send()
    net.drain()


def backward(*ins):
    low, f32 = jnp.bfloat16, jnp.float32
    rows = ins[0].shape[0]
    scratch = [shape for key in stage_keys(range(3)) for shape in came_shapes(LATE, *key)]
    scratch += [shape for key in stage_keys(range(3)) for shape in summed_shapes(LATE, *key)]
    scratch += [
        *[(CTX, 16, HALF_WIDTH)] * 4,
        (CTX, 256, rows),
        (CTX - 1, 256, rows),
        (2 * rows, 1024),
        (2 * rows, HALVES["two"]),
        (2 * rows, 4096),
        (3, 2 * rows, HALVES["three"]),
        (4, 2, 4, 2, 16, HALVES["two"]),
        (4, 2, 4, 2, 64, HALVES["three"]),
    ]
    wide = [
        (128, CTX * rows),
        (128, CTX * rows),
        (STATE, WIDTH),
        (STATE, WIDTH),
        (HEADS, rows, 128),
        (rows, CONV_WIDTH),
        (8, CONV_WIDTH),
        (8, CONV_WIDTH),
        (rows + 8, CONV_WIDTH),
        (rows + 8, CONV_WIDTH),
        (rows, CONV_WIDTH),
        (rows, 128),
    ]
    return call_kernel(
        backward_body,
        "backward",
        3,
        (
            shape_of((rows, COLS), low),
            shape_of((8, CONV_WIDTH), f32),
            shape_of((8, 128), f32),
            shape_of((16, HALVES["two"]), low),
            shape_of((64, HALVES["three"]), low),
        ),
        ins,
        106,
        [*low_scratch(scratch), *[pltpu.VMEM(dims, f32) for dims in wide]],
    )


FIRST = ("one",)


def weight_grads_body(
    norm, grads_one, small, unit_two, unit_three, out_one, out_two, out_three, *rest
):
    came, rest = take(rest, stage_keys(range(3)), FIRST)
    summed, rest = take(rest, stage_keys(range(3)), FIRST)
    both_norm, both_one, own_one, small_in, send_sem, recv_sem = rest
    here, core = coordinates()
    near = neighbours(here, core)
    toks = norm.shape[0]
    sibling = device_of(here, 1 - core)
    meet(all_near(near, core) + [sibling])
    net = Sender(send_sem.at[pl.ds(3, 42)], recv_sem.at[pl.ds(3, 42)])
    mine, theirs = pl.ds(0, toks), pl.ds(toks, toks)
    first = [
        net.push(norm, both_norm.at[theirs], sibling),
        net.push(grads_one.at[:, half_of(1 - core, "one")], both_one.at[theirs], sibling),
        net.push(small, small_in, sibling),
    ]
    both_norm[mine] = norm[...]
    both_one[mine] = grads_one[:, half_of(core, "one")]
    over_z = device_of({**here, "zl": 1 - here["zl"]}, core)
    y, low_z = here["y"], here["zl"]
    late = {"two": out_two, "three": out_three}
    out_two[y, low_z, :, half_of(core, "two")] = unit_two[...]
    out_three[y, low_z, :, half_of(core, "three")] = unit_three[...]

    def pass_on(kind, ref, at_y, at_z, targets):
        piece = ref.at[at_y, at_z, :, half_of(core, kind)]
        return [net.push(piece, piece, target) for target in targets]

    def late_step(at_y, at_z, targets):
        return [
            copy
            for kind, ref in late.items()
            for copy in pass_on(kind, ref, at_y, at_z, targets)
        ]

    to_y = [device_of(at, core) for at in near["y"]]
    late_copies = late_step(y, low_z, [over_z])
    for copy in first:
        copy.wait_recv()

    def block(owner_x, owner_z):
        owner = owner_x * 2 + owner_z
        features = both_norm[:, pl.ds(pl.multiple_of(owner * 128, 128), 128)]
        for low_at, high_at in ((0, 1024), (1024, 2176)):
            found = dot_rows(features, both_one[:, low_at:high_at])
            for unit in range(8):
                rows = found[unit * 16 : unit * 16 + 16]
                if unit == 0 and low_at:
                    extra = (small[owner] + small_in[owner]) * core.astype(jnp.float32)
                    tail = rows[:, 1024:].astype(jnp.float32) + extra
                    rows = jnp.concatenate([rows[:, :1024], tail.astype(jnp.bfloat16)], axis=1)
                own_one[owner_x, owner_z, unit // 2, unit % 2, :, low_at:high_at] = rows

    sums = Sums(net, FIRST, here, near, core, came, summed, (own_one,))

    def turn(e, nothing):
        owner_x = (here["x"] + e + 1) % 4
        block(owner_x, 0)
        block(owner_x, 1)
        for copy in sums.early(e, send_sem, recv_sem):
            copy.start()
        return nothing

    lax.fori_loop(0, 3, turn, 0)

    def own_turn(owner_z, nothing):
        block(here["x"], owner_z)
        return nothing

    lax.fori_loop(0, 2, own_turn, 0)
    sums.send(1, 0)
    sums.send(2, 0)
    for copy in late_copies:
        copy.wait_recv()
    late_copies = late_step(y, slice(None), to_y)
    for e in range(3):
        for copy in sums.early(e, send_sem, recv_sem):
            copy.wait_recv()
    for stage in range(3):
        for part in range(3):
            sums.wait(part)
            sums.add_up(part, stage)
            if stage < 2:
                sums.send(part, stage + 1)
        if stage == 1:
            for copy in late_copies:
                copy.wait_recv()
            late_copies = late_step(slice(None), slice(None), [sibling])
    for part in range(3):
        rows, cols = cut_of("one", part, core)
        out_one[y, low_z, rows, cols] = summed[part, 2][0][...]
    for step in (
        (y, low_z, [over_z]),
        (y, slice(None), to_y),
        (slice(None), slice(None), [sibling]),
    ):
        for copy in pass_on("one", out_one, *step):
            copy.wait_recv()
    for copy in late_copies:
        copy.wait_recv()
    for e in range(3):
        for copy in sums.early(e, send_sem, recv_sem):
            copy.wait_send()
    net.drain()


def sum_weight_grads(norm, grads_one, small, unit_two, unit_three):
    toks = norm.shape[0]
    low = jnp.bfloat16
    scratch = [shape for key in stage_keys(range(3)) for shape in came_shapes(FIRST, *key)]
    scratch += [shape for key in stage_keys(range(3)) for shape in summed_shapes(FIRST, *key)]
    scratch += [
        (2 * toks, 1024),
        (2 * toks, HALVES["one"]),
        (4, 2, 4, 2, 16, HALVES["one"]),
    ]
    return call_kernel(
        weight_grads_body,
        "sum_weight_grads",
        5,
        tuple(
            shape_of((4, 2, UNIT_ROWS[kind], 2 * HALVES[kind]), low)
            for kind in ("one", "two", "three")
        ),
        (norm, grads_one, small, unit_two, unit_three),
        45,
        [*low_scratch(scratch), pltpu.VMEM(small.shape, jnp.float32)],
    )


def local(
    layer_input,
    segment_ids,
    norm_gain,
    w_query,
    w_key,
    w_value,
    w_attn_out,
    w_gate_z,
    w_inner,
    w_step,
    conv_weight,
    conv_bias,
    step_bias,
    decay_log,
    skip_gain,
    mixer_gain,
    w_mixer_out,
    ffn_gain,
    w_gate,
    w_up,
    w_down,
    out_grad,
):
    low = jnp.bfloat16
    tok_rows = layer_input.shape[1]
    ctx_here = lax.axis_index("ctx")
    first_pos = ctx_here * tok_rows
    seg_here = segment_ids[0]
    pos_here = first_pos + jnp.arange(tok_rows, dtype=jnp.int32)
    residual_in = layer_input[0].astype(jnp.float32)
    grad_final = out_grad[0].astype(jnp.float32)
    kv_width = KV_HEADS * HEAD_DIM
    q_width = HEADS * HEAD_DIM
    width_inner = SSM_HEADS * SSM_DIM
    conv_width = width_inner + 2 * STATE
    z_at = q_width + 2 * kv_width
    inner_at = z_at + width_inner
    step_at = inner_at + conv_width

    small = jnp.stack(
        [
            jnp.pad(row, (0, 256 - row.shape[0]))
            for row in (
                *conv_weight,
                conv_bias,
                mixer_gain,
                ffn_gain,
                norm_gain,
                step_bias,
                decay_log,
                skip_gain,
                *[jnp.zeros((256,), low)] * 5,
            )
        ]
    )
    in_one = jnp.concatenate(
        [w_query, w_key, w_value, w_gate_z, w_inner, jnp.pad(w_step, ((0, 0), (0, 232)))], axis=1
    )
    all_one, table, seg_got = gather_weights(
        in_one, small, jnp.broadcast_to(segment_ids, (8, tok_rows))
    )
    full_one = all_one.reshape(FSDP * 128, COLS)
    half_dim = HEAD_DIM // 2
    inverse = rope_base ** (-jnp.arange(half_dim, dtype=jnp.float32) / half_dim)
    angles = pos_here.astype(jnp.float32)[:, None] * inverse[None, :]
    cosine = jnp.tile(jnp.cos(angles), (1, 4))
    sine = jnp.sin(angles)
    sine = jnp.concatenate([-sine, sine, -sine, sine], axis=1)
    normed_low, query, local_kv, gate_z, inner_pre, steps = project(
        residual_in, table, cosine, sine, full_one
    )
    seq_total = CTX * tok_rows
    pos_all = jnp.arange(seq_total, dtype=jnp.int32)
    seg_all = seg_got[:, 0].reshape(seq_total)
    visible = (pos_all[None, :] <= pos_here[:, None]) & (seg_all[None, :] == seg_here[:, None])
    hidden_mask = jnp.where(visible, 0.0, masked_score)

    seg_prior = lax.dynamic_slice_in_dim(seg_all, jnp.maximum(first_pos - 3, 0), 3)
    seg_before = jnp.where(ctx_here > 0, seg_prior, -1)
    seg_ext = jnp.concatenate([seg_before, seg_here])
    columns = [seg_ext[k : k + tok_rows] == seg_here for k in range(CONV - 1)]
    columns += [seg_here == seg_before[2], seg_here == seg_here[-1]]
    columns += [jnp.broadcast_to(seg_here[-1] == seg_before[2], (tok_rows,))]
    masks = jnp.pad(jnp.stack(columns, axis=1).astype(jnp.float32), ((0, 0), (0, 122)))
    order_idx = jnp.arange(tok_rows, dtype=jnp.int32)
    intra = (
        (seg_here[:, None] == seg_here[None, :]) & (order_idx[:, None] >= order_idx[None, :])
    ).astype(jnp.float32)
    (
        kv_all,
        rim_got,
        mixed,
        cumulative,
        sizes,
        entering,
        carried,
        mixer_result,
        decays,
        attended,
        log_total,
        all_two,
        all_three,
    ) = forward(
        query,
        local_kv,
        hidden_mask,
        inner_pre,
        steps,
        masks,
        intra,
        table,
        jnp.concatenate([w_gate, w_up], axis=1),
        jnp.concatenate([w_attn_out, w_mixer_out, w_down], axis=0),
    )
    (
        layer_out,
        grad_middle,
        attn_low,
        mixer_low,
        hidden_low,
        normed_two_low,
        grads_two,
        grads_three,
        grad_out_wide,
        grad_result,
        grad_z,
        grad_gain_two,
        grad_mixer_gain,
    ) = middle_part(
        residual_in,
        grad_final,
        attended,
        mixer_result,
        gate_z,
        table,
        all_two.reshape(FSDP * 128, 2 * HALVES["two"]),
        all_three.reshape(FSDP, OUT_ROWS, 2 * HALVES["three"]),
    )
    grad_gain_two, grad_mixer_gain = grad_gain_two[0], grad_mixer_gain[0]
    grads_one, grad_conv_all, grad_heads, unit_two, unit_three = backward(
        grad_result,
        mixed,
        entering,
        decays,
        query,
        grad_out_wide,
        kv_all,
        hidden_mask,
        log_total,
        normed_two_low,
        grads_two,
        attn_low,
        mixer_low,
        hidden_low,
        grads_three,
        carried,
        cumulative,
        sizes,
        inner_pre,
        rim_got,
        steps,
        masks,
        intra,
        table,
        cosine,
        sine,
        grad_z,
    )
    grad_conv, grad_conv_bias = grad_conv_all[:CONV], grad_conv_all[CONV]
    grad_step_bias = grad_heads[0, :SSM_HEADS]
    grad_decay = grad_heads[1, :SSM_HEADS]
    grad_skip = grad_heads[2, :SSM_HEADS]
    grad_normed_one = right_trans(grads_one, full_one)
    _, pull_one = jax.vjp(rms_scale, residual_in, table[7, : residual_in.shape[1]])
    grad_in_norm, grad_gain_one = pull_one(grad_normed_one)
    input_grad = grad_middle + grad_in_norm

    small_grads = jnp.concatenate(
        [
            grad_gain_one.reshape(FSDP, 128),
            grad_conv.reshape(CONV, FSDP, 224).transpose(1, 0, 2).reshape(FSDP, CONV * 224),
            grad_conv_bias.reshape(FSDP, 224),
            grad_step_bias.reshape(FSDP, 3),
            grad_decay.reshape(FSDP, 3),
            grad_skip.reshape(FSDP, 3),
            grad_mixer_gain.reshape(FSDP, 192),
            grad_gain_two.reshape(FSDP, 128),
            jnp.zeros((FSDP, 2048 - SMALL), jnp.float32),
        ],
        axis=1,
    ).reshape(FSDP, 16, 128)
    sum_one, sum_two, sum_three = sum_weight_grads(
        normed_low, grads_one, small_grads, unit_two, unit_three
    )
    one = sum_one.reshape(128, COLS).astype(jnp.float32)
    two = sum_two.reshape(128, 2 * HALVES["two"]).astype(jnp.float32)
    three = sum_three.reshape(OUT_ROWS, 2 * HALVES["three"]).astype(jnp.float32)
    tiny = one[0:16, PAD_AT:COLS].reshape(-1)
    return (
        layer_out[None],
        input_grad[None],
        tiny[0:128],
        one[:, :q_width],
        one[:, q_width : q_width + kv_width],
        one[:, q_width + kv_width : z_at],
        three[0:64],
        one[:, z_at:inner_at],
        one[:, inner_at:step_at],
        one[:, step_at : step_at + SSM_HEADS],
        tiny[128:1024].reshape(CONV, 224),
        tiny[1024:1248],
        tiny[1248:1251],
        tiny[1251:1254],
        tiny[1254:1257],
        tiny[1257:1449],
        three[64:256],
        tiny[1449:1577],
        two[:, : HALVES["two"]],
        two[:, HALVES["two"] :],
        three[256:512],
    )


def solution(mesh):
    in_specs = (
        P("fsdp", "ctx", None),
        P("fsdp", "ctx"),
        P("fsdp"),
        P("fsdp", None),
        P("fsdp", None),
        P("fsdp", None),
        P("fsdp", None),
        P("fsdp", None),
        P("fsdp", None),
        P("fsdp", None),
        P(None, "fsdp"),
        P("fsdp"),
        P("fsdp"),
        P("fsdp"),
        P("fsdp"),
        P("fsdp"),
        P("fsdp", None),
        P("fsdp"),
        P("fsdp", None),
        P("fsdp", None),
        P("fsdp", None),
        P("fsdp", "ctx", None),
    )
    out_specs = (
        P("fsdp", "ctx", None),
        P("fsdp", "ctx", None),
        P("fsdp"),
        P("fsdp", None),
        P("fsdp", None),
        P("fsdp", None),
        P("fsdp", None),
        P("fsdp", None),
        P("fsdp", None),
        P("fsdp", None),
        P(None, "fsdp"),
        P("fsdp"),
        P("fsdp"),
        P("fsdp"),
        P("fsdp"),
        P("fsdp"),
        P("fsdp", None),
        P("fsdp"),
        P("fsdp", None),
        P("fsdp", None),
        P("fsdp", None),
    )
    return jax.shard_map(local, mesh=mesh, in_specs=in_specs, out_specs=out_specs, check_vma=False)
```

profile of v0, /device:TPU:1, one launch (start us, length us, event | category | flops | bytes accessed | tf_op | source)
XLA Modules:
  0.0 362.6 jit_solution(4276581637174205435)
XLA Ops:
  6.3 1.2 stack.69.small
  7.6 1.2 broadcast_in_dim.40.seg
  11.3 1.0 constant_dynamic-update-slice_fusion.1
  12.5 1.1 copy-done.3
  13.6 45.7 %gather_weights.1 = (bf16[4,2,4,2,16,4352]{5,4,3,2,1,0:T(8,128)(2,1)}, f32[16,1792]{1,0:T(8,128)}, s32[16,8,128]{2,1,0:T(8,128)}) custom-call(bf16[4,2,16,4352]{3,2,1,0:T(8,128)(2,1)} %bitcast.67, bf16[16,256]{1,0:T(8,128)(2,1)} %stack.69.small, s32[8,128]{1,0:T(8,128)} %broadcast_in_dim.40.seg), custom_call_target="tpu_custom_call" | custom-call | tf_op jit(solution)/shard_map/gather_weights/pallas_call | solution.py:110
  61.6 1.3 compare_bitcast_fusion
  67.0 1.1 bitcast_convert_fusion.2
  68.1 6.4 %project.1 = (bf16[128,1024]{1,0:T(8,128)(2,1)}, bf16[8,128,128]{2,1,0:T(8,128)(2,1)}, bf16[128,256]{1,0:T(8,128)(2,1)}, f32[128,1536]{1,0:T(8,128)}, f32[128,1792]{1,0:T(8,128)}, /*index=5*/f32[128,128]{1,0:T(8,128)}) custom-call(f32[128,1024]{1,0:T(8,128)} %get-tuple-element.137.row_in, f32[16,1792]{1,0:T(8,128)} %get-tuple-element.64.table, ...), custom_call_target="tpu_custom_call" | custom-call | tf_op jit(solution)/shard_map/project/pallas_call | solution.py:550
  74.5 1.2 fusion.1.hidden_mask
  75.8 1.1 pad_maximum_fusion
  77.3 1.0 pad_maximum_fusion.1
  78.4 87.4 %forward.1 = (bf16[16,128,256]{2,1,0:T(8,128)(2,1)}, f32[8,1792]{1,0:T(8,128)}, f32[128,1792]{1,0:T(8,128)}, f32[128,128]{1,0:T(8,128)}, f32[128,128]{1,0:T(8,12...) custom-call(bf16[8,128,128]{2,1,0:T(8,128)(2,1)} %get-tuple-element., ...), custom_call_target="tpu_custom_call" | custom-call | tf_op jit(solution)/shard_map/forward/pallas_call | solution.py:110
  165.8 21.9 %middle_part.1 = (bf16[128,1024]{1,0:T(8,128)(2,1)}, f32[128,1024]{1,0:T(8,128)}, bf16[128,512]{1,0:T(8,128)(2,1)}, bf16[128,1536]{1,0:T(8,128)(2,1)}, bf16[128,...) custom-call(f32[128,1024]{1,0:T(8,128)} %get-tuple-element.137.row_i, ...), custom_call_target="tpu_custom_call" | custom-call | tf_op jit(solution)/shard_map/middle_part/pallas_call | solution.py:550
  187.7 83.9 %backward.1 = (bf16[128,4352]{1,0:T(8,128)(2,1)}, f32[8,1792]{1,0:T(8,128)}, f32[8,128]{1,0:T(8,128)}, bf16[16,2048]{1,0:T(8,128)(2,1)}, bf16[64,512]{1,0:T(8,128)(2,1)}) custom-call(f32[128,1536]{1,0:T(8,128)} %get-tuple-element.78.grad, f32[128,1792]{1,0:T(8,128)} %get-tuple-element.79.mixed, f32[128,128]{1,0:T(8,128)} %get-tuple-element.80.entering, ...), custom_call_target="tpu_custom_call" | custom-call | tf_op jit(solution)/shard_map/backward/pallas_call | solution.py:110
  272.5 8.2 %fusion.7 = (f32[1024]{0:T(1024)S(1)}, f32[128]{0:T(128)}, f32[128,1024]{1,0:T(8,128)}) fusion(bf16[1,128,1024]{2,1,0:T(8,128)(2,1)S(1)} %copy-done.1, f32[128]{0:T(128)S(1)} %fusion.11, f32[1024]{0:T(1024)S(1)} %bitcast.73, bf16[128,4352]{1,0:T(8,128)(2,1)} %get-tuple-element.96.grads_one, bf16[1024,4352]{1,0:T(8,128)(2,1)} %bitcast.60), kind=kOutput, calls=%fused_computation.17 | convolution fusion | flops 1141767040 | bytes 10822656 | tf_op jit(solution)/shard_map/dot_general | solution.py:33
  284.5 60.6 %sum_weight_grads.1 = (bf16[4,2,16,4352]{3,2,1,0:T(8,128)(2,1)}, bf16[4,2,16,4096]{3,2,1,0:T(8,128)(2,1)}, bf16[4,2,64,1024]{3,2,1,0:T(8,128)(2,1)}) custom-call(bf16[128,1024]{1,0:T(8,128)(2,1)} %get-tuple-element.97.norm, bf16[128,4352]{1,0:T(8,128)(2,1)} %get-tuple-element.96.grads_one, f32[8,16,128]{2,1,0:T(8,128)} %bitcast.69, ...), custom_call_target="tpu_custom_call" | custom-call | tf_op jit(solution)/shard_map/sum_weight_grads/pallas_call | solution.py:110
  345.1 1.4 bitcast_convert_fusion.1
  346.5 1.5 fusion.14
  348.4 1.0 slice.156
  349.3 1.0 slice.155
  351.1 0.9 slice.165
  354.8 1.5 copy.77
  359.9 1.1 slice.169
  361.6 1.0 fusion.3
  (112 shorter events, 26.6 us)
Async XLA Ops:
  0.7 11.6 %copy-start.9 = (bf16[128,1792]{1,0:T(8,128)(2,1)S(1)}, bf16[128,1792]{1,0:T(8,128)(2,1)}, u32[]{:S(2)}) copy-start(bf16[128,1792]{1,0:T(8,128)(2,1)} %param.30) | copy-start | bytes 1376260
  0.7 11.7 %copy-start.15 = (bf16[128,24]{0,1:T(8,128)(2,1)S(1)}, bf16[128,24]{0,1:T(8,128)(2,1)}, u32[]{:S(2)}) copy-start(bf16[128,24]{0,1:T(8,128)(2,1)} %param.31) | copy-start | bytes 18436
  12.3 48.0 %copy-start.13 = (s32[1,128]{1,0:T(1,128)S(1)}, s32[1,128]{1,0:T(1,128)}, u32[]{:S(2)}) copy-start(s32[1,128]{1,0:T(1,128)} %param.23) | copy-start | bytes 1540
  12.4 54.6 %copy-start.1 = (bf16[1,128,1024]{2,1,0:T(8,128)(2,1)S(1)}, bf16[1,128,1024]{2,1,0:T(8,128)(2,1)}, u32[]{:S(2)}) copy-start(bf16[1,128,1024]{2,1,0:T(8,128)(2,1)} %param.22) | copy-start | bytes 786436
  12.4 54.6 %copy-start.11 = (bf16[1,128,1024]{2,1,0:T(8,128)(2,1)S(1)}, bf16[1,128,1024]{2,1,0:T(8,128)(2,1)}, u32[]{:S(2)}) copy-start(bf16[1,128,1024]{2,1,0:T(8,128)(2,1)} %param.43) | copy-start | bytes 786436
  12.5 1.1 copy-start.3
  74.5 1.2 copy-start.6
  74.5 1.3 copy-start.7
  75.8 1.1 copy-start.8
  75.8 1.5 copy-start.10
  75.8 1.6 copy-start.12
  272.5 8.2 %copy-start.14 = (f32[8,1792]{1,0:T(8,128)S(1)}, f32[8,1792]{1,0:T(8,128)}, u32[]{:S(2)}) copy-start(f32[8,1792]{1,0:T(8,128)} %get-tuple-element.98) | copy-start | bytes 172036
  346.5 1.7 copy-start.4
  349.3 1.5 copy-start
  359.3 2.3 copy-start.2
  359.3 2.3 copy-start.5
where the time goes:
time: 364 us; the launch traced here: 363 us
  Pallas kernels  306 us (84%)
  local copies, waits for them, and re-layouts  34.8 us (10%)
  other arithmetic  11.4 us (3%)
  matrix products  8.21 us (2%)
    pallas_call x4, Pallas kernels, call_kernel(): pl.pallas_call(body, name=name, out_shape=outs, in_specs=[spec(k in far_i...  278 us
    pallas_call x2, Pallas kernels, plain_kernel(): pl.pallas_call(body, name=name, out_shape=outs, in_specs=[pl.BlockSpec(me...  28.3 us
    dot_general x1, matrix products, right_trans(): lax.dot_general(left_side, right_side, (((1,), (1,)), ((), ())), preferre...  8.21 us
    unnamed x40, local copies, waits for them, and re-layouts  8.21 us

commit v1 on v0

--- a/solution.py
+++ b/solution.py
@@ -207,6 +207,7 @@
         return copies
 
     def stage(self, number, ins=None):
+        jobs = []
         for part, order in enumerate(ORDERS):
             steps = order[::-1]
             dim, fixed = steps[number], steps[number:]
@@ -221,19 +222,17 @@
                     ]
                     for kind in self.outs
                 ]
-            self.pending[part] = [
-                self.net.push(src, ref, device_of(at, self.core))
-                for at in self.near[dim]
-                for src, ref in zip(sources, refs)
-            ]
-            if number == 2:
+            jobs.append((self.near[dim], sources, refs))
+            self.pending[part] = []
+        for e in range(3):
+            for part, (near, sources, refs) in enumerate(jobs):
+                self.pending[part] += [
+                    self.net.push(src, ref, device_of(near[e], self.core))
+                    for src, ref in zip(sources, refs)
+                ]
+        if number == 2:
+            for _, _, refs in jobs:
                 self.crossing += [self.net.push(ref, ref, self.sibling) for ref in refs]
-
-    def settle(self):
-        for part in range(3):
-            for copy in self.pending[part]:
-                copy.wait_recv()
-        self.pending = [[], [], []]
 
     def finish(self):
         kinds = len(self.outs)
@@ -256,63 +255,7 @@
     ]
 
 
-def gather_body(in_one, small, seg, out_one, table, seg_all, got_small, own_sem, send_sem, recv_sem):
-    here, core = coordinates()
-    near = neighbours(here, core)
-    f = here["x"] * 2 + here["zh"]
-    c = at_ctx(here["y"], here["zl"], core)
-    small_peers = [{"fsdp": (f + d) % FSDP} for d in range(1, FSDP)]
-    meet(
-        all_near(near, core)
-        + [{"fsdp": (here["x"] + e) % 4 * 2 + 1 - here["zh"]} for e in range(1, 4)]
-        + ctx_peers(c)
-    )
-    net = Sender(send_sem, recv_sem)
-    gather = Gather(net, {"one": out_one}, here, near, core)
-    gather.stage(0, {"one": in_one})
-    own = gather.own({"one": in_one}, own_sem)
-    for copy in own:
-        copy.start()
-    tiny = [net.push(small, got_small.at[f], peer) for peer in small_peers]
-    got_small[f] = small[...]
-    tiny += [net.push(seg, seg_all.at[c], peer) for peer in ctx_peers(c)]
-    seg_all[c] = seg[...]
-    for copy in own:
-        copy.wait()
-    gather.stage(1)
-    gather.stage(2)
-    for copy in tiny:
-        copy.wait_recv()
-    table[...] = jnp.zeros_like(table)
-    for k in range(FSDP):
-        piece = got_small[k].astype(jnp.float32)
-        for first, last, width in TABLE:
-            table[first:last, k * width : k * width + width] = piece[first:last, :width]
-    table[9:10] = jnp.exp(table[9:10])
-    table[11:12, :WIDTH] = expand(table[10:11, 0:128])
-    gather.finish()
-    net.drain()
-
-
 TABLE = ((0, 5, 224), (5, 6, 192), (6, 8, 128), (8, 11, 3))
-
-
-def gather_weights(in_one, small, seg):
-    return call_kernel(
-        gather_body,
-        "gather_weights",
-        0,
-        (
-            *gather_shapes(["one"]),
-            shape_of((16, CONV_WIDTH), jnp.float32),
-            shape_of((CTX, *seg.shape), seg.dtype),
-        ),
-        (in_one.reshape(4, 2, 16, COLS), small, seg),
-        61,
-        (pltpu.VMEM((FSDP, 16, 256), jnp.bfloat16), pltpu.SemaphoreType.DMA((2,))),
-        (0,),
-        (0,),
-    )
 
 
 def ctx_peers(c):
@@ -384,17 +327,48 @@
     )
 
 
+def masks_from(seg, seg_cols, seg_all, c, hidden_mask, masks, intra):
+    rows = seg_cols.shape[0]
+    row = lax.broadcasted_iota(jnp.int32, (rows, 128), 0)
+    lane = lax.broadcasted_iota(jnp.int32, (rows, 128), 1)
+    here = seg_cols[:, 3:4]
+    before = jnp.where(c > 0, seg_all[(c + CTX - 1) % CTX][0:1], -1)
+    found = jnp.zeros((rows, 128), jnp.float32)
+    for tap in range(CONV - 1):
+        earlier = jnp.broadcast_to(seg_cols[:, tap : tap + 1], (rows, 128))
+        for t in range(CONV - 1 - tap):
+            at = 125 + t + tap
+            earlier = jnp.where(row == t, before[:, at : at + 1], earlier)
+        found = jnp.where((lane == tap) & (earlier == here), 1.0, found)
+    last, prior = seg[0:1, 127:128], before[:, 127:128]
+    found = jnp.where((lane == 3) & (here == prior), 1.0, found)
+    found = jnp.where((lane == 4) & (here == last), 1.0, found)
+    masks[...] = jnp.where((lane == 5) & (last == prior), 1.0, found)
+    intra[...] = jnp.where((row >= lane) & (here == seg[0:1]), 1.0, 0.0)
+    for k in range(CTX):
+        seen = (here == seg_all[k][0:1]) & (lane + k * rows <= row + c * rows)
+        hidden_mask[:, k * rows : (k + 1) * rows] = jnp.where(seen, 0.0, masked_score)
+
+
 def forward_body(
+    row_in,
+    cosine,
+    sine,
+    small,
+    seg,
+    seg_cols,
+    in_one,
+    in_two,
+    in_three,
+    norm_low,
     query,
-    kv,
-    hidden_mask,
+    gate_z,
     inner,
     steps,
+    table,
+    hidden_mask,
     masks,
     intra,
-    table,
-    in_two,
-    in_three,
     kv_all,
     rim_all,
     mixed,
@@ -406,8 +380,12 @@
     decays,
     attended,
     log_total,
+    out_one,
     out_two,
     out_three,
+    kv,
+    got_small,
+    seg_all,
     states,
     inside,
     extended,
@@ -422,23 +400,57 @@
 ):
     here, core = coordinates()
     near = neighbours(here, core)
-    c = at_ctx(here["y"], here["zl"], core)
+    y, low_z = here["y"], here["zl"]
+    c = at_ctx(y, low_z, core)
+    f = here["x"] * 2 + here["zh"]
     peers = ctx_peers(c)
-    rows = kv_all.shape[1]
-    meet(peers + all_near(near, core))
+    rows = row_in.shape[0]
+    small_peers = [{"fsdp": (f + d) % FSDP} for d in range(1, FSDP)]
+    meet(
+        peers
+        + all_near(near, core)
+        + [{"fsdp": (here["x"] + e) % 4 * 2 + 1 - here["zh"]} for e in range(1, 4)]
+    )
     net = Sender(send_sem, recv_sem)
-    rim_copy = net.push(inner.at[pl.ds(rows - 8, 8)], rim_all, peers[0])
-    key_copies = [net.push(kv, kv_all.at[c], peer) for peer in peers]
+    early = Gather(net, {"one": out_one}, here, near, core)
+    early.stage(0, {"one": in_one})
+    tiny = [net.push(small, got_small.at[f], peer) for peer in small_peers]
+    tiny += [net.push(seg, seg_all.at[c], peer) for peer in peers]
     ins = {"two": in_two, "three": in_three}
-    gather = Gather(net, {"two": out_two, "three": out_three}, here, near, core)
-    gather.stage(0, ins)
-    own = gather.own(ins, own_sem)
-    for copy in own:
+    late = Gather(net, {"two": out_two, "three": out_three}, here, near, core)
+    own = early.own({"one": in_one}, own_sem.at[pl.ds(0, 1)])
+    own_late = late.own(ins, own_sem.at[pl.ds(1, 2)])
+    for copy in own + own_late:
         copy.start()
-    kv_all[c] = kv[...]
+    got_small[f] = small[...]
+    seg_all[c] = seg[...]
     for copy in own:
         copy.wait()
-    gather.stage(1)
+    early.stage(1)
+    early.stage(2)
+    late.stage(0, ins)
+    for copy in tiny:
+        copy.wait_recv()
+    table[...] = jnp.zeros_like(table)
+    for k in range(FSDP):
+        piece = got_small[k].astype(jnp.float32)
+        for first, last, width in TABLE:
+            table[first:last, k * width : k * width + width] = piece[first:last, :width]
+    table[9:10] = jnp.exp(table[9:10])
+    table[11:12, :WIDTH] = expand(table[10:11, 0:128])
+    masks_from(seg, seg_cols, seg_all, c, hidden_mask, masks, intra)
+    early.finish()
+    for copy in own_late:
+        copy.wait()
+    late.stage(1)
+    project_body(
+        row_in, table, cosine, sine, out_one, norm_low, query, kv, gate_z, inner, steps
+    )
+    rim_copy = net.push(inner.at[pl.ds(rows - 8, 8)], rim_all, peers[0])
+    over_z = device_of({**here, "zl": 1 - low_z}, core)
+    sibling = device_of(here, 1 - core)
+    kv_all[y, low_z, core] = kv[...]
+    to_z = net.push(kv, kv_all.at[y, low_z, core], over_z)
     rim_copy.wait_recv()
     mixer_parts_body(
         inner,
@@ -463,13 +475,17 @@
         copies.append(net.push(decay, decays.at[c], peer))
     parts[c] = states[c]
     decays[c] = decay[...]
-    gather.stage(2)
-    for copy in key_copies:
+    to_z.wait_recv()
+    pair = kv_all.at[y, :, core]
+    to_y = [net.push(pair, pair, device_of(at, core)) for at in near["y"]]
+    for copy in to_y:
         copy.wait_recv()
+    whole = kv_all.at[:, :, core]
+    net.push(whole, whole, sibling).wait_recv()
 
     def head(h, nothing):
-        keys = kv_all[:, :, 0:128].reshape(CTX * rows, 128)
-        values = kv_all[:, :, 128:256].reshape(CTX * rows, 128)
+        keys = kv_all[:, :, :, :, 0:128].reshape(CTX * rows, 128)
+        values = kv_all[:, :, :, :, 128:256].reshape(CTX * rows, 128)
         scores = across(query[h], keys) + hidden_mask[...]
         row_max = jnp.max(scores, axis=-1, keepdims=True)
         weights = jnp.exp(scores - row_max)
@@ -481,12 +497,12 @@
         log_total[h] = jnp.broadcast_to(row_max + jnp.log(row_sum), (rows, 128))
         return nothing
 
-    lax.fori_loop(0, 3, head, 0)
     for copy in copies:
         copy.wait_recv()
     scan_rows(range(CTX), decays, parts, carries)
     back = send_back(net, c, peers, carries, came_back)
-    lax.fori_loop(3, HEADS, head, 0)
+    late.stage(2)
+    lax.fori_loop(0, HEADS, head, 0)
     for copy in back:
         copy.wait_recv()
     unpack(came_back, carried)
@@ -494,19 +510,28 @@
     result[...] = inside[...] + expand(entering[...]) * jnp.dot(
         output_map, carried[...].astype(jnp.bfloat16), preferred_element_type=jnp.float32
     )
-    gather.finish()
+    late.finish()
     net.drain()
 
 
-def forward(query, kv, hidden_mask, inner, steps, masks, intra, table, two, three):
-    rows = query.shape[1]
+def forward(row_in, cosine, sine, small, seg, seg_cols, one, two, three):
+    rows, dim = row_in.shape
     f32, low = jnp.float32, jnp.bfloat16
     return call_kernel(
         forward_body,
         "forward",
         1,
         (
-            shape_of((CTX, *kv.shape), kv.dtype),
+            shape_of((rows, dim), low),
+            shape_of((HEADS, rows, 128), low),
+            shape_of((rows, WIDTH), f32),
+            shape_of((rows, CONV_WIDTH), f32),
+            shape_of((rows, 128), f32),
+            shape_of((16, CONV_WIDTH), f32),
+            shape_of((rows, CTX * rows), f32),
+            shape_of((rows, 128), f32),
+            shape_of((rows, rows), f32),
+            shape_of((4, 2, 2, rows, 256), low),
             shape_of((8, CONV_WIDTH), f32),
             shape_of((rows, CONV_WIDTH), f32),
             shape_of((rows, 128), f32),
@@ -517,32 +542,34 @@
             shape_of((CTX, 8, 128), f32),
             shape_of((HEADS, rows, 128), low),
             shape_of((HEADS, rows, 128), f32),
-            *gather_shapes(["two", "three"]),
+            *gather_shapes(["one", "two", "three"]),
         ),
         (
-            query,
-            kv,
-            hidden_mask,
-            inner,
-            steps,
-            masks,
-            intra,
-            table,
+            row_in,
+            cosine,
+            sine,
+            small,
+            seg,
+            seg_cols,
+            one.reshape(4, 2, 16, 2 * HALVES["one"]),
             two.reshape(4, 2, 16, 2 * HALVES["two"]),
             three.reshape(4, 2, 64, 2 * HALVES["three"]),
         ),
-        139,
+        190,
         (
+            pltpu.VMEM((rows, 256), low),
+            pltpu.VMEM((FSDP, 16, 256), low),
+            pltpu.VMEM((CTX, 8, 128), jnp.int32),
             pltpu.VMEM((CTX, 16, HALF_WIDTH), low),
             pltpu.VMEM((rows, WIDTH), f32),
             pltpu.VMEM((rows + 8, CONV_WIDTH), f32),
             pltpu.VMEM((STATE, WIDTH), f32),
             *[pltpu.VMEM((CTX, 16, HALF_WIDTH), low)] * 3,
             pltpu.VMEM((8, 128), f32),
-            pltpu.SemaphoreType.DMA((2,)),
+            pltpu.SemaphoreType.DMA((3,)),
         ),
-        (8, 9),
-        (11, 12),
+        (6, 7, 8),
+        (21, 22),
     )
 
 
@@ -628,7 +655,8 @@
     norm_low[...] = normed
 
     def part(first, last):
-        return jnp.dot(normed, weights[:, first:last], preferred_element_type=jnp.float32)
+        piece = weights[:, :, :, :, :, first:last].reshape(values.shape[1], last - first)
+        return jnp.dot(normed, piece, preferred_element_type=jnp.float32)
 
     def turn(both):
         return both * cosine[...] + swap_quarters(both) * sine[...]
@@ -643,24 +671,6 @@
     for at in range(0, CONV_WIDTH, 256):
         inner[:, at : at + 256] = part(INNER_AT + at, INNER_AT + at + 256)
     steps[...] = part(STEP_AT, STEP_AT + 128)
-
-
-def project(row_in, table, cosine, sine, weights):
-    rows, dim = row_in.shape
-    f32, low = jnp.float32, jnp.bfloat16
-    return plain_kernel(
-        project_body,
-        "project",
-        (
-            shape_of((rows, dim), low),
-            shape_of((HEADS, rows, 128), low),
-            shape_of((rows, 256), low),
-            shape_of((rows, WIDTH), f32),
-            shape_of((rows, CONV_WIDTH), f32),
-            shape_of((rows, 128), f32),
-        ),
-        (row_in, table, cosine, sine, weights),
-    )
 
 
 def mixer_parts_body(
@@ -1159,6 +1169,14 @@
     toks = norm.shape[0]
     mine, theirs = pl.ds(0, toks), pl.ds(toks, toks)
     other = 1 - core
+    output_map = mixed[:, WIDTH + STATE :].astype(jnp.bfloat16)
+    wide_states[...] = down(
+        output_map, (expand(entering[...]) * grad[...]).astype(jnp.bfloat16)
+    )
+    pack(wide_states, states)
+    copies = [
+        net.push(states.at[(c + e + 1) % CTX], parts.at[c], peer) for e, peer in enumerate(peers)
+    ]
     first = [
         net.push(norm, both_norm.at[theirs], sibling),
         net.push(grads_two.at[:, half_of(other, "two")], both_two.at[theirs], sibling),
@@ -1173,15 +1191,11 @@
     both_act[mine, 512:2048] = acts_mixer[...]
     both_act[mine, 2048:4096] = acts_hidden[...]
     both_three[:, mine] = grads_three[:, :, half_of(core, "three")]
-    output_map = mixed[:, WIDTH + STATE :].astype(jnp.bfloat16)
-    wide_states[...] = down(
-        output_map, (expand(entering[...]) * grad[...]).astype(jnp.bfloat16)
-    )
-    pack(wide_states, states)
-    copies = [
-        net.push(states.at[(c + e + 1) % CTX], parts.at[c], peer) for e, peer in enumerate(peers)
-    ]
     parts[c] = states[c]
+    for copy in copies:
+        copy.wait_recv()
+    scan_rows(range(CTX - 1, -1, -1), decays, parts, carries)
+    back = send_back(net, c, peers, carries, came_back)
     for copy in first:
         copy.wait_recv()
 
@@ -1217,10 +1231,6 @@
     block(here["x"])
     sums.send(1, 0)
     sums.send(2, 0)
-    for copy in copies:
-        copy.wait_recv()
-    scan_rows(range(CTX - 1, -1, -1), decays, parts, carries)
-    back = send_back(net, c, peers, carries, came_back)
     key_sum[...] = jnp.zeros_like(key_sum)
     value_sum[...] = jnp.zeros_like(value_sum)
 
@@ -1559,37 +1569,24 @@
     in_one = jnp.concatenate(
         [w_query, w_key, w_value, w_gate_z, w_inner, jnp.pad(w_step, ((0, 0), (0, 232)))], axis=1
     )
-    all_one, table, seg_got = gather_weights(
-        in_one, small, jnp.broadcast_to(segment_ids, (8, tok_rows))
-    )
-    full_one = all_one.reshape(FSDP * 128, COLS)
     half_dim = HEAD_DIM // 2
     inverse = rope_base ** (-jnp.arange(half_dim, dtype=jnp.float32) / half_dim)
     angles = pos_here.astype(jnp.float32)[:, None] * inverse[None, :]
     cosine = jnp.tile(jnp.cos(angles), (1, 4))
     sine = jnp.sin(angles)
     sine = jnp.concatenate([-sine, sine, -sine, sine], axis=1)
-    normed_low, query, local_kv, gate_z, inner_pre, steps = project(
-        residual_in, table, cosine, sine, full_one
-    )
-    seq_total = CTX * tok_rows
-    pos_all = jnp.arange(seq_total, dtype=jnp.int32)
-    seg_all = seg_got[:, 0].reshape(seq_total)
-    visible = (pos_all[None, :] <= pos_here[:, None]) & (seg_all[None, :] == seg_here[:, None])
-    hidden_mask = jnp.where(visible, 0.0, masked_score)
-
-    seg_prior = lax.dynamic_slice_in_dim(seg_all, jnp.maximum(first_pos - 3, 0), 3)
-    seg_before = jnp.where(ctx_here > 0, seg_prior, -1)
-    seg_ext = jnp.concatenate([seg_before, seg_here])
-    columns = [seg_ext[k : k + tok_rows] == seg_here for k in range(CONV - 1)]
-    columns += [seg_here == seg_before[2], seg_here == seg_here[-1]]
-    columns += [jnp.broadcast_to(seg_here[-1] == seg_before[2], (tok_rows,))]
-    masks = jnp.pad(jnp.stack(columns, axis=1).astype(jnp.float32), ((0, 0), (0, 122)))
-    order_idx = jnp.arange(tok_rows, dtype=jnp.int32)
-    intra = (
-        (seg_here[:, None] == seg_here[None, :]) & (order_idx[:, None] >= order_idx[None, :])
-    ).astype(jnp.float32)
+    seg_early = jnp.concatenate([jnp.full((CONV - 1,), -2, jnp.int32), seg_here])
+    seg_cols = jnp.stack([seg_early[k : k + tok_rows] for k in range(CONV)], axis=1)
     (
+        normed_low,
+        query,
+        gate_z,
+        inner_pre,
+        steps,
+        table,
+        hidden_mask,
+        masks,
+        intra,
         kv_all,
         rim_got,
         mixed,
@@ -1601,20 +1598,22 @@
         decays,
         attended,
         log_total,
+        all_one,
         all_two,
         all_three,
     ) = forward(
-        query,
-        local_kv,
-        hidden_mask,
-        inner_pre,
-        steps,
-        masks,
-        intra,
-        table,
+        residual_in,
+        cosine,
+        sine,
+        small,
+        jnp.broadcast_to(segment_ids, (8, tok_rows)),
+        jnp.pad(seg_cols, ((0, 0), (0, 128 - CONV))),
+        in_one,
         jnp.concatenate([w_gate, w_up], axis=1),
         jnp.concatenate([w_attn_out, w_mixer_out, w_down], axis=0),
     )
+    kv_all = kv_all.reshape(CTX, tok_rows, 256)
+    full_one = all_one.reshape(FSDP * 128, COLS)
     (
         layer_out,
         grad_middle,

time: 364 us -> 333 us (0.915)
  Pallas kernels: 306 us -> 285 us
  local copies, waits for them, and re-layouts: 34.8 us -> 29.4 us
    pallas_call x4 -> x3, Pallas kernels: 278 us -> 263 us  [call_kernel(): pl.pallas_call(body, name=name, out_shape=outs, in_specs=[spec(k in far_i...]
    pallas_call x2 -> x1, Pallas kernels: 28.3 us -> 21.9 us  [plain_kernel(): pl.pallas_call(body, name=name, out_shape=outs, in_specs=[pl.BlockSpec(me...]
    unnamed x40 -> x48, local copies, waits for them, and re-layouts: 8.21 us -> 4.01 us
where the time goes in v1:
time: 333 us; the launch traced here: 332 us
  Pallas kernels  285 us (86%)
  local copies, waits for them, and re-layouts  29.4 us (9%)
  other arithmetic  8.52 us (3%)
  matrix products  8.18 us (2%)
    pallas_call x3, Pallas kernels, call_kernel(): pl.pallas_call(body, name=name, out_shape=outs, in_specs=[spec(k in far_i...  263 us
    pallas_call x1, Pallas kernels, plain_kernel(): pl.pallas_call(body, name=name, out_shape=outs, in_specs=[pl.BlockSpec(me...  21.9 us
    dot_general x1, matrix products, right_trans(): lax.dot_general(left_side, right_side, (((1,), (1,)), ((), ())), preferre...  8.18 us

profile of v1, /device:TPU:1, one launch (start us, length us, event | category | flops | bytes accessed | tf_op | source)
XLA Modules:
  0.0 331.9 jit_solution(2000346244649032926)
XLA Ops:
  0.7 0.9 slice_reduce_fusion.2
  6.3 1.2 stack.67.small
  7.6 0.8 fusion.7
  10.2 0.8 pad_maximum_fusion.2.sine
  11.7 1.1 bitcast_convert_fusion.2
  14.6 1.0 pad_maximum_fusion
  15.7 1.0 pad_maximum_fusion.1
  16.7 119.7 %forward.1 = (bf16[128,1024]{1,0:T(8,128)(2,1)}, bf16[8,128,128]{2,1,0:T(8,128)(2,1)}, f32[128,1536]{1,0:T(8,128)}, f32[128,1792]{1,0:T(8,128)}, f32[128,128]{1,...) custom-call(f32[128,1024]{1,0:T(8,128)} %get-tuple-element.133.row_i, ...), custom_call_target="tpu_custom_call" | custom-call | tf_op jit(solution)/shard_map/forward/pallas_call | solution.py:110
  136.4 21.9 %middle_part.1 = (bf16[128,1024]{1,0:T(8,128)(2,1)}, f32[128,1024]{1,0:T(8,128)}, bf16[128,512]{1,0:T(8,128)(2,1)}, bf16[128,1536]{1,0:T(8,128)(2,1)}, bf16[128,...) custom-call(f32[128,1024]{1,0:T(8,128)} %get-tuple-element.133.row_i, ...), custom_call_target="tpu_custom_call" | custom-call | tf_op jit(solution)/shard_map/middle_part/pallas_call | solution.py:577
  158.3 80.2 %backward.1 = (bf16[128,4352]{1,0:T(8,128)(2,1)}, f32[8,1792]{1,0:T(8,128)}, f32[8,128]{1,0:T(8,128)}, bf16[16,2048]{1,0:T(8,128)(2,1)}, bf16[64,512]{1,0:T(8,128)(2,1)}) custom-call(f32[128,1536]{1,0:T(8,128)} %get-tuple-element.73.grad, f32[128,1792]{1,0:T(8,128)} %get-tuple-element.74.mixed, f32[128,128]{1,0:T(8,128)} %get-tuple-element.75.entering, ...), custom_call_target="tpu_custom_call" | custom-call | tf_op jit(solution)/shard_map/backward/pallas_call | solution.py:110
  238.6 0.8 slice.105
  239.5 8.2 %fusion.5 = (f32[1024]{0:T(1024)S(1)}, f32[128]{0:T(128)}, f32[128,1024]{1,0:T(8,128)}) fusion(bf16[1,128,1024]{2,1,0:T(8,128)(2,1)S(1)} %copy-done.1, f32[128]{0:T(128)S(1)} %fusion.10, f32[1024]{0:T(1024)S(1)} %bitcast.65, bf16[128,4352]{1,0:T(8,128)(2,1)} %get-tuple-element.97.grads_one, bf16[1024,4352]{1,0:T(8,128)(2,1)} %bitcast.51), kind=kOutput, calls=%fused_computation.14 | convolution fusion | flops 1141767040 | bytes 10822656 | tf_op jit(solution)/shard_map/dot_general | solution.py:33
  248.0 0.8 slice_reduce_fusion.6
  249.0 0.8 slice_reduce_fusion.1
  249.9 0.8 slice.112
  251.4 63.0 %sum_weight_grads.1 = (bf16[4,2,16,4352]{3,2,1,0:T(8,128)(2,1)}, bf16[4,2,16,4096]{3,2,1,0:T(8,128)(2,1)}, bf16[4,2,64,1024]{3,2,1,0:T(8,128)(2,1)}) custom-call(bf16[128,1024]{1,0:T(8,128)(2,1)} %get-tuple-element.99.norm, bf16[128,4352]{1,0:T(8,128)(2,1)} %get-tuple-element.97.grads_one, f32[8,16,128]{2,1,0:T(8,128)} %bitcast.61, ...), custom_call_target="tpu_custom_call" | custom-call | tf_op jit(solution)/shard_map/sum_weight_grads/pallas_call | solution.py:110
  314.4 1.4 bitcast_convert_fusion.1
  315.9 1.5 fusion.12
  317.7 1.0 slice.141
  318.7 1.0 slice.140
  320.5 0.9 slice.150
  324.1 1.5 copy.75
  329.2 1.1 slice.154
  331.0 1.0 fusion.1
  (110 shorter events, 18.6 us)
Async XLA Ops:
  0.7 11.1 %copy-start.1 = (bf16[1,128,1024]{2,1,0:T(8,128)(2,1)S(1)}, bf16[1,128,1024]{2,1,0:T(8,128)(2,1)}, u32[]{:S(2)}) copy-start(bf16[1,128,1024]{2,1,0:T(8,128)(2,1)} %param.22) | copy-start | bytes 786436
  0.7 11.1 %copy-start.12 = (bf16[1,128,1024]{2,1,0:T(8,128)(2,1)S(1)}, bf16[1,128,1024]{2,1,0:T(8,128)(2,1)}, u32[]{:S(2)}) copy-start(bf16[1,128,1024]{2,1,0:T(8,128)(2,1)} %param.43) | copy-start | bytes 786436
  9.8 3.0 copy-start.19
  9.8 3.6 %copy-start.14 = (bf16[128,512]{1,0:T(8,128)(2,1)S(1)}, bf16[128,512]{1,0:T(8,128)(2,1)}, u32[]{:S(2)}) copy-start(bf16[128,512]{1,0:T(8,128)(2,1)} %param.25) | copy-start | bytes 393220
  10.9 2.5 copy-start.15
  10.9 2.6 copy-start.16
  11.0 2.5 copy-start.11
  11.7 1.8 copy-start.9
  12.8 0.8 copy-start.18
  13.4 1.0 copy-start.6
  13.4 1.2 copy-start.7
  13.6 2.1 copy-start.8
  13.6 2.1 copy-start.10
  13.6 2.0 copy-start.13
  13.8 2.9 copy-start.3
  239.5 8.2 %copy-start.17 = (f32[8,1792]{1,0:T(8,128)S(1)}, f32[8,1792]{1,0:T(8,128)}, u32[]{:S(2)}) copy-start(f32[8,1792]{1,0:T(8,128)} %get-tuple-element.100) | copy-start | bytes 172036
  315.9 1.7 copy-start.4
  318.7 1.5 copy-start
  328.7 2.2 copy-start.2
  328.7 2.2 copy-start.5

commit v2 on v1

--- a/solution.py
+++ b/solution.py
@@ -1510,6 +1510,31 @@
     )
 
 
+def first_norm_grads_body(grads_one, weights, row_in, grad_middle, table, input_grad, gain_grad):
+    dim = row_in.shape[1]
+    grad_norm = across(grads_one[...], weights[...])
+    values = row_in[...]
+    scale = lax.rsqrt(mean_last(values * values) + epsilon)
+    weighted = grad_norm * table[7:8, 0:dim]
+    input_grad[...] = (
+        grad_middle[...]
+        + scale * weighted
+        - values * (scale * scale * scale) * mean_last(values * weighted)
+    )
+    gain_grad[...] = jnp.broadcast_to(
+        jnp.sum(grad_norm * values * scale, axis=0, keepdims=True), gain_grad.shape
+    )
+
+
+def first_norm_grads(grads_one, weights, row_in, grad_middle, table):
+    return plain_kernel(
+        first_norm_grads_body,
+        "first_norm_grads",
+        (shape_of(row_in.shape, jnp.float32), shape_of((8, row_in.shape[1]), jnp.float32)),
+        (grads_one, weights, row_in, grad_middle, table),
+    )
+
+
 def local(
     layer_input,
     segment_ids,
@@ -1550,22 +1575,20 @@
     inner_at = z_at + width_inner
     step_at = inner_at + conv_width
 
-    small = jnp.stack(
-        [
-            jnp.pad(row, (0, 256 - row.shape[0]))
-            for row in (
-                *conv_weight,
-                conv_bias,
-                mixer_gain,
-                ffn_gain,
-                norm_gain,
-                step_bias,
-                decay_log,
-                skip_gain,
-                *[jnp.zeros((256,), low)] * 5,
-            )
-        ]
-    )
+    small_rows = (
+        *conv_weight,
+        conv_bias,
+        mixer_gain,
+        ffn_gain,
+        norm_gain,
+        step_bias,
+        decay_log,
+        skip_gain,
+    )
+    small = jnp.concatenate(
+        [piece for row in small_rows for piece in (row, jnp.zeros((256 - row.shape[0],), low))]
+        + [jnp.zeros((5 * 256,), low)]
+    ).reshape(16, 256)
     in_one = jnp.concatenate(
         [w_query, w_key, w_value, w_gate_z, w_inner, jnp.pad(w_step, ((0, 0), (0, 232)))], axis=1
     )
@@ -1672,10 +1695,10 @@
     grad_step_bias = grad_heads[0, :SSM_HEADS]
     grad_decay = grad_heads[1, :SSM_HEADS]
     grad_skip = grad_heads[2, :SSM_HEADS]
-    grad_normed_one = right_trans(grads_one, full_one)
-    _, pull_one = jax.vjp(rms_scale, residual_in, table[7, : residual_in.shape[1]])
-    grad_in_norm, grad_gain_one = pull_one(grad_normed_one)
-    input_grad = grad_middle + grad_in_norm
+    input_grad, grad_gain_one = first_norm_grads(
+        grads_one, full_one, residual_in, grad_middle, table
+    )
+    grad_gain_one = grad_gain_one[0]
 
     small_grads = jnp.concatenate(
         [

time: 333 us -> 330 us (level)
  matrix products: 8.18 us -> 0 us
  Pallas kernels: 285 us -> 293 us
    dot_general x1 -> x0, matrix products: 8.18 us -> none  [right_trans(): lax.dot_general(left_side, right_side, (((1,), (1,)), ((), ())), preferre...]
    pallas_call x1 -> x2, Pallas kernels: 21.9 us -> 29.8 us  [plain_kernel(): pl.pallas_call(body, name=name, out_shape=outs, in_specs=[pl.BlockSpec(me...]
    concatenate x0 -> x1, local copies, waits for them, and re-layouts: none -> 4.77 us  [local(): jnp.concatenate([piece for row in small_rows for piece in (row, jnp.zeros...]
    pad x11 -> x0, local copies, waits for them, and re-layouts: 4.64 us -> none  [local(): jnp.pad(row, (0, 256 - row.shape[0]))]
where the time goes in v2:
time: 330 us; the launch traced here: 329 us
  Pallas kernels  293 us (89%)
  local copies, waits for them, and re-layouts  27.4 us (8%)
  other arithmetic  7.85 us (2%)
    pallas_call x3, Pallas kernels, call_kernel(): pl.pallas_call(body, name=name, out_shape=outs, in_specs=[spec(k in far_i...  263 us
    pallas_call x2, Pallas kernels, plain_kernel(): pl.pallas_call(body, name=name, out_shape=outs, in_specs=[pl.BlockSpec(me...  29.8 us

profile of v2, /device:TPU:1, one launch (start us, length us, event | category | flops | bytes accessed | tf_op | source)
XLA Modules:
  0.0 328.9 jit_solution(3920371768746495806)
XLA Ops:
  0.7 0.9 slice_reduce_fusion.2
  1.6 4.8 %concatenate.22 = bf16[4096]{0:T(1024)(128)(2,1)S(1)} concatenate(bf16[224]{0:T(256)(128)(2,1)S(1)} %get-tuple-element.118, bf16[32]{0:T(256)(128)(2,1)S(1)} %broadcast.51, bf16[224]{0:T(256)(128)(2,1)S(1)} %get-tuple-element.117, bf16[32]{0:T(256)(128)(2,1)S(1)} %broadcast.51, bf16[224]{0:T(256)(128)(2,1)S(1)} %get-tuple-element.119, bf16[32]{0:T(256)(128)(2,1)S(1)} %broadcast.51, ...), dimensions={0} | concatenate | bytes 16384 | tf_op jit(solution)/shard_map/concatenate | solution.py:1588
  6.9 0.8 fusion.1
  9.6 0.8 pad_maximum_fusion.2.sine
  10.3 2.2 bitcast_convert_fusion.2
  12.6 0.7 copy.71.cosine
  15.1 1.0 pad_maximum_fusion
  16.1 1.0 pad_maximum_fusion.1
  17.2 119.7 %forward.1 = (bf16[128,1024]{1,0:T(8,128)(2,1)}, bf16[8,128,128]{2,1,0:T(8,128)(2,1)}, f32[128,1536]{1,0:T(8,128)}, f32[128,1792]{1,0:T(8,128)}, f32[128,128]{1,...) custom-call(f32[128,1024]{1,0:T(8,128)} %get-tuple-element.134.row_i, ...), custom_call_target="tpu_custom_call" | custom-call | tf_op jit(solution)/shard_map/forward/pallas_call | solution.py:110
  136.9 21.9 %middle_part.1 = (bf16[128,1024]{1,0:T(8,128)(2,1)}, f32[128,1024]{1,0:T(8,128)}, bf16[128,512]{1,0:T(8,128)(2,1)}, bf16[128,1536]{1,0:T(8,128)(2,1)}, bf16[128,...) custom-call(f32[128,1024]{1,0:T(8,128)} %get-tuple-element.134.row_i, ...), custom_call_target="tpu_custom_call" | custom-call | tf_op jit(solution)/shard_map/middle_part/pallas_call | solution.py:577
  158.8 80.2 %backward.1 = (bf16[128,4352]{1,0:T(8,128)(2,1)}, f32[8,1792]{1,0:T(8,128)}, f32[8,128]{1,0:T(8,128)}, bf16[16,2048]{1,0:T(8,128)(2,1)}, bf16[64,512]{1,0:T(8,128)(2,1)}) custom-call(f32[128,1536]{1,0:T(8,128)} %get-tuple-element.74.grad, f32[128,1792]{1,0:T(8,128)} %get-tuple-element.75.mixed, f32[128,128]{1,0:T(8,128)} %get-tuple-element.76.entering, ...), custom_call_target="tpu_custom_call" | custom-call | tf_op jit(solution)/shard_map/backward/pallas_call | solution.py:110
  239.0 7.9 %first_norm_grads.1 = (f32[128,1024]{1,0:T(8,128)}, f32[8,1024]{1,0:T(8,128)}) custom-call(bf16[128,4352]{1,0:T(8,128)(2,1)} %get-tuple-element.98.grads_one, bf16[1024,4352]{1,0:T(8,128)(2,1)} %bitcast.43, f32[128,1024]{1,0:T(8,128)} %get-tuple-element.134.row_in, f32[128,1024]{1,0:T(8,128)} %get-tuple-element.100.grad_middle, ...), custom_call_target="tpu_custom_call" | custom-call | tf_op jit(solution)/shard_map/first_norm_grads/pallas_call | solution.py:577
  246.9 0.8 slice.105
  248.0 0.8 slice_reduce_fusion.6
  249.0 0.8 slice_reduce_fusion.1
  250.0 0.8 slice.112
  251.5 63.0 %sum_weight_grads.1 = (bf16[4,2,16,4352]{3,2,1,0:T(8,128)(2,1)}, bf16[4,2,16,4096]{3,2,1,0:T(8,128)(2,1)}, bf16[4,2,64,1024]{3,2,1,0:T(8,128)(2,1)}) custom-call(bf16[128,1024]{1,0:T(8,128)(2,1)} %get-tuple-element.102.norm, bf16[128,4352]{1,0:T(8,128)(2,1)} %get-tuple-element.98.grads_one, f32[8,16,128]{2,1,0:T(8,128)} %bitcast.53, ...), custom_call_target="tpu_custom_call" | custom-call | tf_op jit(solution)/shard_map/sum_weight_grads/pallas_call | solution.py:110
  314.5 1.4 bitcast_convert_fusion.1
  315.9 1.5 fusion.5
  317.8 1.0 slice.141
  318.8 1.0 slice.140
  320.5 0.9 slice.150
  321.5 0.7 slice.136
  327.8 1.1 slice.154
  (81 shorter events, 12.3 us)
Async XLA Ops:
  9.2 4.1 %copy-start.15 = (s32[1,128]{1,0:T(1,128)S(1)}, s32[1,128]{1,0:T(1,128)}, u32[]{:S(2)}) copy-start(s32[1,128]{1,0:T(1,128)} %param.23) | copy-start | bytes 1540
  9.2 4.7 %copy-start.10 = (bf16[128,512]{1,0:T(8,128)(2,1)S(1)}, bf16[128,512]{1,0:T(8,128)(2,1)}, u32[]{:S(2)}) copy-start(bf16[128,512]{1,0:T(8,128)(2,1)} %param.25) | copy-start | bytes 393220
  10.3 3.6 %copy-start.11 = (bf16[128,128]{1,0:T(8,128)(2,1)S(1)}, bf16[128,128]{1,0:T(8,128)(2,1)}, u32[]{:S(2)}) copy-start(bf16[128,128]{1,0:T(8,128)(2,1)} %param.26) | copy-start | bytes 98308
  10.3 3.6 %copy-start.12 = (bf16[128,128]{1,0:T(8,128)(2,1)S(1)}, bf16[128,128]{1,0:T(8,128)(2,1)}, u32[]{:S(2)}) copy-start(bf16[128,128]{1,0:T(8,128)(2,1)} %param.27) | copy-start | bytes 98308
  10.3 3.7 %copy-start.8 = (bf16[128,1536]{1,0:T(8,128)(2,1)S(1)}, bf16[128,1536]{1,0:T(8,128)(2,1)}, u32[]{:S(2)}) copy-start(bf16[128,1536]{1,0:T(8,128)(2,1)} %param.29) | copy-start | bytes 1179652
  12.5 1.5 copy-start.6
  12.6 1.5 copy-start.14
  13.9 1.0 copy-start.3
  13.9 1.2 copy-start.4
  14.1 2.1 copy-start.5
  14.1 2.1 copy-start.7
  14.1 2.0 copy-start.9
  14.3 2.9 copy-start.1
  239.0 8.7 %copy-start.13 = (f32[8,1792]{1,0:T(8,128)S(1)}, f32[8,1792]{1,0:T(8,128)}, u32[]{:S(2)}) copy-start(f32[8,1792]{1,0:T(8,128)} %get-tuple-element.104) | copy-start | bytes 172036
  315.9 1.7 copy-start.2
  318.8 1.5 copy-start
